TPU v7x, 32 devices: a whole 2x2x4 slice. The times are simulated.
32 devices in a mesh: dp: 8 (over z, x), seq: 4 (over y, core).
Axes of the slice: x: 2, y: 2, z: 4, core: 2. Of those that a mesh axis runs over, the one named last changes fastest.
Arguments:
- tokens: bfloat16 [8, 8192, 768], P('dp', 'seq'), may hold values from -6 to 6
- cotangent: bfloat16 [8, 8192, 768], P('dp', 'seq'), may hold values from -6 to 6
- norm_gain: bfloat16 [768], P(('dp', 'seq')), may hold values from 0.5 to 1.5
- in_weight: bfloat16 [768, 3352], P(('dp', 'seq')), may hold values from -0.21875 to 0.21875
- conv_weight: bfloat16 [1792, 4], P(('dp', 'seq')), may hold values from -3 to 3
- conv_bias: bfloat16 [1792], P(('dp', 'seq')), may hold values from -3 to 3
- step_bias: float32 [24], replicated, may hold values from -9 to -4
- decay_log: float32 [24], replicated, may hold values from 0 to 1.5
- skip_gain: float32 [24], replicated, may hold values from 0.5 to 1.5
- gate_gain: bfloat16 [1536], P(('dp', 'seq')), may hold values from 0.5 to 1.5
- out_weight: bfloat16 [1536, 768], P(('dp', 'seq')), may hold values from -0.15625 to 0.15625
Outputs:
- mixed: bfloat16 [8, 8192, 768], P('dp', 'seq')
- tokens_grad: bfloat16 [8, 8192, 768], P('dp', 'seq')
- norm_gain_grad: float32 [768], P(('dp', 'seq'))
- in_weight_grad: float32 [768, 3352], P(('dp', 'seq'))
- conv_weight_grad: float32 [1792, 4], P(('dp', 'seq'))
- conv_bias_grad: float32 [1792], P(('dp', 'seq'))
- step_bias_grad: float32 [24], replicated
- decay_log_grad: float32 [24], replicated
- skip_gain_grad: float32 [24], replicated
- gate_gain_grad: float32 [1536], P(('dp', 'seq'))
- out_weight_grad: float32 [1536, 768], P(('dp', 'seq'))
All inputs are finite; a program needn't handle non-finite values.
Results may differ from a plain program's by a relative error of at most 0.012.
Values may be sent and summed in bfloat16 or wider, within the bound.
A program may use at most 384 MiB of HBM per device.

v0:
```python
import functools

import jax
import jax.numpy as jnp
import numpy as np
from jax import lax
from jax.experimental import pallas as pl
from jax.experimental.pallas import tpu as pltpu
from jax.sharding import PartitionSpec as P

D = 768
HEADS = 24
HEADDIM = 64
NSTATE = 128
CONV = 4
BLOCK = 128
DI = 1536
CH = 1792
PAIRS = HEADS // 2
EPS = 1e-05
LOG2E = 1.4426950408889634
F32 = jnp.float32
BF16 = jnp.bfloat16
NT = (((1,), (1,)), ((), ()))
VMEM_LIMIT = 60 * 1024 * 1024


def dot(a, b):
    return jnp.dot(a, b, preferred_element_type=F32)


def dot_nt(a, b):
    return lax.dot_general(a, b, NT, preferred_element_type=F32)


def dot_exact(a, b):
    return jnp.dot(a, b, preferred_element_type=F32, precision=lax.Precision.HIGHEST)


def sigmoid(v):
    return 0.5 * jnp.tanh(0.5 * v) + 0.5


def iota(shape, dim):
    return lax.broadcasted_iota(jnp.int32, shape, dim)


def lane_lo():
    return iota((BLOCK, BLOCK), 1) < HEADDIM


def expand_pair(x, j, lo):
    rows = x.shape[0]
    a = jnp.broadcast_to(x[:, 2 * j : 2 * j + 1], (rows, BLOCK))
    b = jnp.broadcast_to(x[:, 2 * j + 1 : 2 * j + 2], (rows, BLOCK))
    return jnp.where(lo, a, b), a, b


def block_diag(v):
    lo = iota(v.shape, 1) < HEADDIM
    zero = jnp.zeros_like(v)
    return jnp.concatenate([jnp.where(lo, v, zero), jnp.where(lo, zero, v)], axis=0)


def pair(j):
    return slice(j * BLOCK, (j + 1) * BLOCK)


MESH = pl.DeviceIdType.MESH
ANY = pl.BlockSpec(memory_space=pl.ANY)
WC = CH + BLOCK
TN = (((0,), (0,)), ((), ()))


def dot_tn(a, b):
    return lax.dot_general(a, b, TN, preferred_element_type=F32)


def sizes():
    return {"z": lax.axis_size("dp") // 2, "x": 2, "y": lax.axis_size("seq") // 2, "c": 2}


def place():
    dp, seq = lax.axis_index("dp"), lax.axis_index("seq")
    return {"z": dp // 2, "x": lax.rem(dp, 2), "y": seq // 2, "c": lax.rem(seq, 2)}


def device(at):
    return {"dp": at["z"] * 2 + at["x"], "seq": at["y"] * 2 + at["c"]}


def peers(at, axis):
    n = sizes()[axis]
    return [dict(at, **{axis: lax.rem(at[axis] + o, n)}) for o in range(1, n)]


def greet(at, axes, by=0):
    sem = pltpu.get_barrier_semaphore()
    count = 0
    for axis in axes:
        for peer in peers(at, axis):
            pl.semaphore_signal(sem, inc=1, device_id=device(peer), device_id_type=MESH)
            count += 1
    if not by:
        pl.semaphore_wait(sem, count)
        return
    seq, n = lax.axis_index("seq"), lax.axis_size("seq")

    @pl.when((seq + by >= 0) & (seq + by < n))
    def _():
        pl.semaphore_signal(sem, inc=1, device_id={"seq": seq + by}, device_id_type=MESH)

    heard = (seq - by >= 0) & (seq - by < n)

    @pl.when(heard)
    def _():
        pl.semaphore_wait(sem, count + 1)

    @pl.when(jnp.logical_not(heard))
    def _():
        pl.semaphore_wait(sem, count)


def greet_neighbours():
    seq, n = lax.axis_index("seq"), lax.axis_size("seq")
    sem = pltpu.get_barrier_semaphore()

    @pl.when(seq > 0)
    def _():
        pl.semaphore_signal(sem, inc=1, device_id={"seq": seq - 1}, device_id_type=MESH)

    @pl.when(seq < n - 1)
    def _():
        pl.semaphore_signal(sem, inc=1, device_id={"seq": seq + 1}, device_id_type=MESH)

    @pl.when((seq > 0) & (seq < n - 1))
    def _():
        pl.semaphore_wait(sem, 2)

    @pl.when((seq == 0) | (seq == n - 1))
    def _():
        pl.semaphore_wait(sem, 1)


def remote(src, dst, send, recv, peer):
    return pltpu.make_async_remote_copy(
        src_ref=src, dst_ref=dst, send_sem=send, recv_sem=recv, device_id=device(peer), device_id_type=MESH
    )


class Gather:
    def __init__(self, slab, spot, order, sems):
        self.slab, self.spot, self.order = slab, spot, order
        self.send, self.recv = sems
        self.at = place()

    def copies(self, stage):
        at, (a, b) = self.at, self.order
        n = sizes()
        out = []
        every = slice(None)
        nz = n["z"] - 1
        if stage == 0:
            for o, peer in enumerate(peers(at, "z")):
                out.append((self.slab, self.spot(at), o, peer))
        elif stage == 1:
            index = dict(at, z=every)
            out.append((self.spot(index), self.spot(index), nz, peers(at, a)[0]))
        elif stage == 2:
            index = dict(at, z=every)
            index[a] = every
            for o, peer in enumerate(peers(at, b)):
                out.append((self.spot(index), self.spot(index), nz + 1 + o, peer))
            out.append((self.spot(index), self.spot(index), nz + 1 + n[b] - 1, peers(at, "c")[0]))
        else:
            for o in range(1, n[b]):
                index = dict(at, z=every)
                index[a] = every
                index[b] = lax.rem(at[b] + o, n[b])
                out.append((self.spot(index), self.spot(index), nz + 1 + n[b] + o - 1, peers(at, "c")[0]))
        return [remote(s, d, self.send.at[k], self.recv.at[k], p) for s, d, k, p in out]

    def start(self, stage):
        for c in self.copies(stage):
            c.start()

    def wait(self, stage):
        for c in self.copies(stage):
            c.wait()


def spots(buf, lanes=slice(None)):
    return lambda index: buf.at[index["z"], index["x"], index["y"], index["c"], :, lanes]


def gather_sems():
    count = sizes()["z"] + 2 * sizes()["y"] + 4
    return [pltpu.SemaphoreType.DMA((count,)), pltpu.SemaphoreType.DMA((count,))]


class Scatter:
    def __init__(self, grads, order, scratch, own=None, local=None):
        self.grads, self.order, self.own_ref, self.local = grads, order, own, local
        self.rc, self.r1, self.r2, self.rz, self.send, self.recv = scratch
        self.at = place()
        self.own = self

    def spot(self, z, x, y):
        if self.own_ref is not None:
            return self.own_ref.at[z, x, y]
        return self.grads.at[z, x, y, self.at["c"]]

    def add(self, z, x, y, got):
        mine = self.spot(z, x, y)
        mine[...] = (mine[...].astype(F32) + got.astype(F32)).astype(BF16)

    def copies(self, stage):
        at, (a, b) = self.at, self.order
        every = slice(None)
        out = []

        def spot(index):
            return self.spot(index["z"], index["x"], index["y"])

        if stage == 0:
            out.append((self.grads.at[:, :, :, 1 - at["c"]], self.rc, 0, peers(at, "c")[0]))
        elif stage == 1:
            index = {"z": every, "x": every, "y": every}
            index[a] = 1 - at[a]
            out.append((spot(index), self.r1, 1, peers(at, a)[0]))
        elif stage == 2:
            index = {"z": every, a: at[a], b: 1 - at[b]}
            out.append((spot(index), self.r2, 2, peers(at, b)[0]))
        else:
            for o, peer in enumerate(peers(at, "z")):
                out.append((self.spot(peer["z"], at["x"], at["y"]), self.rz.at[o], 3 + o, peer))
        return [remote(s, d, self.send.at[k], self.recv.at[k], p) for s, d, k, p in out]

    def mine(self):
        return pltpu.make_async_copy(self.grads.at[:, :, :, self.at["c"]], self.own_ref, self.local)

    def start(self, stage):
        if stage == 0 and self.own_ref is not None:
            self.mine().start()
        for c in self.copies(stage):
            c.start()

    def finish(self, stage):
        at, (a, b) = self.at, self.order
        for c in self.copies(stage):
            c.wait()
        nz = sizes()["z"]
        if stage == 0:
            if self.own_ref is not None:
                self.mine().wait()

            def body(z, _):
                for x in range(2):
                    for y in range(2):
                        self.add(z, x, y, self.rc[z, x, y])
                return _

        elif stage == 1:

            def body(z, _):
                for k in range(2):
                    index = {a: at[a], b: k}
                    self.add(z, index["x"], index["y"], self.r1[z, k])
                return _

        else:

            def body(z, _):
                self.add(z, at["x"], at["y"], self.r2[z])
                return _

        lax.fori_loop(0, nz, body, 0)

    def result(self):
        for c in self.copies(3):
            c.wait()
        total = self.spot(self.at["z"], self.at["x"], self.at["y"])[...].astype(F32)
        for o in range(sizes()["z"] - 1):
            total = total + self.rz[o].astype(F32)
        return total


def scatter_scratch(rows, width):
    nz = sizes()["z"]
    return [
        pltpu.VMEM((nz, 2, 2, rows, width), BF16), pltpu.VMEM((nz, 2, rows, width), BF16),
        pltpu.VMEM((nz, rows, width), BF16), pltpu.VMEM((nz - 1, rows, width), BF16),
        pltpu.SemaphoreType.DMA((nz + 2,)), pltpu.SemaphoreType.DMA((nz + 2,)),
    ]


NSC = 6


def own_scratch(rows, width):
    return [pltpu.VMEM((sizes()["z"], 2, 2, rows, width), BF16), pltpu.SemaphoreType.DMA(())]


class Chain:
    def __init__(self, leave, inc, decay, bufs, reverse):
        self.leave, self.inc, self.decay, self.reverse = leave, inc, decay, reverse
        self.got, self.put, self.send, self.recv = bufs
        self.n = lax.axis_size("seq")
        seq = lax.axis_index("seq")
        self.rank = self.n - 1 - seq if reverse else seq
        self.to = seq - 1 if reverse else seq + 1

    def copy(self):
        return pltpu.make_async_remote_copy(
            src_ref=self.put, dst_ref=self.got, send_sem=self.send, recv_sem=self.recv,
            device_id={"seq": self.to}, device_id_type=MESH,
        )

    def step(self, k):
        @pl.when(self.rank == k)
        def _():
            if k == 0:
                self.inc[...] = jnp.zeros_like(self.inc)
                self.put[...] = self.leave[...].astype(BF16)
            else:
                self.copy().wait_recv()
                got = self.got[...].astype(F32)
                self.inc[...] = got
                if k < self.n - 1:
                    self.put[...] = (got * self.decay[0:1] + self.leave[...]).astype(BF16)
            if k < self.n - 1:
                self.copy().start()

    def done(self):
        @pl.when(self.rank < self.n - 1)
        def _():
            self.copy().wait_send()


def chain_scratch():
    return [
        pltpu.VMEM((NSTATE, DI), BF16), pltpu.VMEM((NSTATE, DI), BF16), pltpu.SemaphoreType.DMA(()),
        pltpu.SemaphoreType.DMA(()),
    ]


def expand_row(row, dst):
    lo = iota((8, BLOCK), 1) < HEADDIM
    wide = jnp.broadcast_to(row, (8, BLOCK))
    for j in range(PAIRS):
        dst[:, pair(j)] = expand_pair(wide, j, lo)[0]


CHUNKS = ((0, 512), (512, 512), (1024, 512), (1536, 384))
ORDERS = ("xy", "yx", "xy", "yx")


def gate_kernel(normed_ref, wg_ref, cot_ref, wo_ref, gain_ref, leave_ref, tot_ref, gate_ref, ng_ref, inc_ref, decay, *bufs):
    i = pl.program_id(0)
    chain = Chain(leave_ref, inc_ref, decay, bufs, False)
    last = pl.num_programs(0) - 1

    @pl.when(i == 0)
    def _():
        expand_row(jnp.exp2(tot_ref[0:1]), decay)
        greet_neighbours()
        chain.step(0)

    for c in range(DI // 256):
        cs = slice(c * 256, (c + 1) * 256)
        gate_ref[:, cs] = dot(normed_ref[...], wg_ref[:, cs]).astype(BF16)
        ng_ref[:, cs] = (dot_nt(cot_ref[...], wo_ref[cs, :]) * gain_ref[1:2, cs]).astype(BF16)
    for k in range(1, chain.n):
        @pl.when(i == (0, 2, 3)[min(k, 3) - 1])
        def _():
            chain.step(k)

    @pl.when(i == last)
    def _():
        chain.done()


def gate_pass(normed, wg, cot, wo, gain, leave, tot, T=512):
    L = normed.shape[0]
    row = lambda w: pl.BlockSpec((T, w), lambda i: (i, 0))
    return pl.pallas_call(
        gate_kernel,
        grid=(L // T,),
        in_specs=[
            row(D), full((D, DI)), row(D), full((DI, D)), full((8, DI)), full((NSTATE, DI)), full((8, BLOCK)),
        ],
        out_specs=[row(DI), row(DI), full((NSTATE, DI))],
        out_shape=[sds((L, DI), BF16), sds((L, DI), BF16), sds((NSTATE, DI), F32)],
        scratch_shapes=[pltpu.VMEM((8, DI), F32)] + chain_scratch(),
        compiler_params=params(collective_id=2),
        name="gate_pass",
    )(normed, wg, cot, wo, gain, leave, tot)


def grads_kernel(nout_ref, cot_ref, xt_ref, ggrad_ref, back_ref, tot_ref, gout_ref, ggate_ref, inc_ref, decay, *bufs):
    i = pl.program_id(0)
    chain = Chain(back_ref, inc_ref, decay, bufs, True)
    last = pl.num_programs(0) - 1

    @pl.when(i == 0)
    def _():
        expand_row(jnp.exp2(tot_ref[0:1]), decay)
        greet_neighbours()
        chain.step(0)

    gout_ref[...] = dot_tn(nout_ref[...], cot_ref[...]).astype(BF16)
    ggate_ref[...] = dot(xt_ref[...], ggrad_ref[...]).astype(BF16)
    for k in range(1, chain.n):
        @pl.when(i == (0, 3, 5)[min(k, 3) - 1])
        def _():
            chain.step(k)

    @pl.when(i == last)
    def _():
        chain.done()


def grads_pass(nout, cot, xt, ggrad, back, tot):
    L = nout.shape[0]
    col = lambda w: pl.BlockSpec((L, w), lambda i: (0, i))
    return pl.pallas_call(
        grads_kernel,
        grid=(6,),
        in_specs=[
            col(256), full((L, D)), pl.BlockSpec((128, L), lambda i: (i, 0)), full((L, DI)), full((NSTATE, DI)),
            full((8, BLOCK)),
        ],
        out_specs=[
            pl.BlockSpec((256, D), lambda i: (i, 0)), pl.BlockSpec((128, DI), lambda i: (i, 0)), full((NSTATE, DI)),
        ],
        out_shape=[sds((DI, D), BF16), sds((D, DI), BF16), sds((NSTATE, DI), F32)],
        scratch_shapes=[pltpu.VMEM((8, DI), F32)] + chain_scratch(),
        compiler_params=params(collective_id=3),
        name="grads_pass",
    )(nout, cot, xt, ggrad, back, tot)


def last_kernel(
    T, xt_any, pg_any, wg_any, wc_any, tail_ref, ggrad_ref, tok_ref, cot_ref, gain_ref, small_ref,
    tgrad_ref, gout_ref, sums_ref, xt, wg, wc, pg, g0, g1, g2, g3, lsem, smalls, ssend, srecv, *scratch,
):
    i = pl.program_id(0)
    nc = len(CHUNKS)
    grads = (g0, g1, g2, g3)
    sc = [Scatter(grads[k], ORDERS[k][::-1], scratch[NSC * k : NSC * k + NSC]) for k in range(nc)]
    dp, seq = lax.axis_index("dp"), lax.axis_index("seq")
    n_dp, n_seq = lax.axis_size("dp"), lax.axis_size("seq")
    total = n_dp * n_seq
    me = dp * n_seq + seq
    L = pg.shape[0]

    whole = ((xt_any, xt), (wg_any, wg), (wc_any, wc))

    def load(k):
        if k >= nc:
            return pltpu.make_async_copy(*whole[k - nc], lsem.at[k])
        lanes = pl.ds(CHUNKS[k][0], CHUNKS[k][1])
        return pltpu.make_async_copy(pg_any.at[:, lanes], pg.at[:, lanes], lsem.at[k])

    def far(o):
        r = lax.rem(me + o, total)
        return {"dp": r // n_seq, "seq": lax.rem(r, n_seq)}

    def small(o):
        r = lax.rem(me + o, total)
        return pltpu.make_async_remote_copy(
            src_ref=small_ref.at[r], dst_ref=smalls.at[o - 1], send_sem=ssend.at[o - 1], recv_sem=srecv.at[o - 1],
            device_id=far(o), device_id_type=MESH,
        )

    @pl.when(i == 0)
    def _():
        load(nc).start()
        load(0).start()
        sem = pltpu.get_barrier_semaphore()
        for o in range(1, total):
            pl.semaphore_signal(sem, inc=1, device_id=far(o), device_id_type=MESH)

    for k in range(nc):
        @pl.when(i == k)
        def _():
            lane, width = CHUNKS[k]
            if k == 0:
                load(nc).wait()
            load(k).wait()
            if k + 1 < nc:
                load(k + 1).start()
            if k >= nc - 2:
                load(nc + 1 + k - (nc - 2)).start()
            skip = BLOCK if k == 0 else 0
            pg[L - 16 :, lane + skip : lane + width] = tail_ref[:, lane + skip : lane + width]
            rows = grads[k].shape[4]
            for q in range(2):
                half = D // 2
                g = dot(xt[q * half : (q + 1) * half], pg[:, lane : lane + width])
                for r in range(half // rows):
                    s = r + q * (half // rows)
                    grads[k][s // 8, (s // 4) % 2, (s // 2) % 2, s % 2] = g[r * rows : (r + 1) * rows].astype(BF16)
            if k == 0:
                pl.semaphore_wait(pltpu.get_barrier_semaphore(), total - 1)
                sc[0].start(0)
                for o in range(1, total):
                    small(o).start()
            else:
                sc[k - 1].finish(0)
                sc[k - 1].start(1)
                sc[k].start(0)

    @pl.when(i >= nc)
    def _():
        r0 = pl.multiple_of((i - nc) * T, T)

        @pl.when(i == nc)
        def _():
            load(nc + 1).wait()
            load(nc + 2).wait()

        u = dot_nt(ggrad_ref[...], wg[...]) + dot_nt(pg[pl.ds(r0, T), :], wc[...])
        u = u * gain_ref[0:1]
        x = tok_ref[...].astype(F32)
        inv = lax.rsqrt(jnp.mean(x * x, axis=-1, keepdims=True) + EPS)
        xi = x * inv
        coef = inv * jnp.mean(u * xi, axis=-1, keepdims=True)
        tgrad_ref[...] = (cot_ref[...].astype(F32) + inv * u - xi * coef).astype(BF16)

    def after(step, what):
        @pl.when(i == step)
        def _():
            for k, stage in what:
                sc[k].finish(stage)
                sc[k].start(stage + 1)

    after(nc + 1, [(3, 0)])
    after(nc + 3, [(0, 1)])
    after(nc + 4, [(1, 1)])
    after(nc + 5, [(2, 1)])
    after(nc + 6, [(3, 1), (0, 2)])
    after(nc + 7, [(1, 2), (2, 2), (3, 2)])

    @pl.when(i == pl.num_programs(0) - 1)
    def _():
        for o in range(1, total):
            small(o).wait()
        acc = small_ref[me]
        for o in range(1, total):
            acc = acc + smalls[o - 1]
        sums_ref[...] = acc
        for k in range(nc):
            lane, width = CHUNKS[k]
            gout_ref[:, lane : lane + width] = sc[k].result()


def last_pass(xt, pg, tail, ggrad, tok, cot, wg, wc, gain, small):
    L = tok.shape[0]
    T = L // 8
    n = sizes()
    nc = len(CHUNKS)
    total = lax.axis_size("dp") * lax.axis_size("seq")
    rows = D // total
    row = lambda w: pl.BlockSpec((T, w), lambda i: (jnp.maximum(i - nc, 0), 0))
    scratch = []
    for _, w in CHUNKS:
        scratch += scatter_scratch(rows, w)
    return pl.pallas_call(
        functools.partial(last_kernel, T),
        grid=(nc + L // T,),
        in_specs=[
            ANY, ANY, ANY, ANY, once((16, WC)), row(DI), row(D), row(D), once((8, D)), once((total, 8, BLOCK)),
        ],
        out_specs=[row(D), full((rows, WC)), full((8, BLOCK))],
        out_shape=[sds((L, D), BF16), sds((rows, WC), F32), sds((8, BLOCK), F32)],
        scratch_shapes=[
            pltpu.VMEM((D, L), BF16), pltpu.VMEM((D, DI), BF16), pltpu.VMEM((D, WC), BF16), pltpu.VMEM((L, WC), BF16),
        ]
        + [pltpu.VMEM((n["z"], 2, n["y"], 2, rows, w), BF16) for _, w in CHUNKS]
        + [
            pltpu.SemaphoreType.DMA((nc + 3,)), pltpu.VMEM((total - 1, 8, BLOCK), F32),
            pltpu.SemaphoreType.DMA((total - 1,)), pltpu.SemaphoreType.DMA((total - 1,)),
        ] + scratch,
        compiler_params=params(collective_id=5),
        name="last_pass",
    )(xt, pg, wg, wc, tail, ggrad, tok, cot, gain, small)


def finish_kernel(
    gate_ref, conv_ref, out_ref, sums_ref, w_ref, wo_ref, gain_ref, ggain_ref, tgrad_ref,
    in_grad, ngain, ggain, taps, bias, step, decay, skip, out_grad, tgrad_out,
):
    tgrad_out[...] = tgrad_ref[...]

    @pl.when(pl.program_id(0) == 0)
    def _():
        finish_small(
            gate_ref, conv_ref, out_ref, sums_ref, w_ref, wo_ref, gain_ref, ggain_ref, in_grad, ngain, ggain, taps, bias,
            step, decay, skip, out_grad,
        )


def finish_small(
    gate_ref, conv_ref, out_ref, sums_ref, w_ref, wo_ref, gain_ref, ggain_ref,
    in_grad, ngain, ggain, taps, bias, step, decay, skip, out_grad,
):
    conv = conv_ref[...]
    raw = jnp.concatenate([gate_ref[...], conv[:, BLOCK:], conv[:, :HEADS]], axis=1)
    in_grad[...] = raw
    ngain[...] = jnp.sum(raw * w_ref[...].astype(F32), axis=1) / gain_ref[...]
    o = out_ref[...]
    out_grad[...] = o
    ggain[...] = jnp.sum(o * wo_ref[...].astype(F32), axis=1) / ggain_ref[...]
    s = sums_ref[...]
    n = bias.shape[0]
    taps[...] = s.T[:n, :CONV]
    bias[...] = s[4, :n]
    step[...] = s[7, :HEADS]
    decay[...] = s[7, HEADS : 2 * HEADS]
    skip[...] = s[7, 2 * HEADS : 3 * HEADS]


def finish_pass(gate_cols, conv_cols, out_raw, sums, w, wo, gain, ggain, tgrad, channels):
    vec = lambda n: sds((n,), F32)
    rows = pl.BlockSpec((512, D), lambda i: (i, 0))
    small = [
        sds(w.shape, F32), vec(w.shape[0]), vec(wo.shape[0]), sds((channels, CONV), F32),
        vec(channels), vec(HEADS), vec(HEADS), vec(HEADS), sds(out_raw.shape, F32),
    ]
    ins = (gate_cols, conv_cols, out_raw, sums, w, wo, gain, ggain)
    return pl.pallas_call(
        finish_kernel,
        grid=(tgrad.shape[0] // 512,),
        in_specs=[once(x.shape) for x in ins] + [rows],
        out_specs=[once(x.shape) for x in small] + [rows],
        out_shape=small + [sds(tgrad.shape, BF16)],
        name="finish_pass",
    )(*ins, tgrad)


def rms_rows(tok, gain):
    x = tok.astype(F32)
    return (x * lax.rsqrt(jnp.mean(x * x, axis=-1, keepdims=True) + EPS) * gain).astype(BF16)


def first_kernel(
    T, win_ref, small, tok_any, so_ref,
    xhat_any, xt_any, wc_any, p_any, hp_ref, conv_ref, gain_ref, row_ref,
    act_ref, slope_ref, dt_ref, cum_ref, sig_ref, bst_ref, leave_ref, tot_ref, bg_ref, bo_ref,
    slab, tok, halo, xhat, xt, wc, wide, p, smalls, b0, b1, b2, b3, ext, state, weighted, lsem, hsend, hrecv, ssend, srecv,
    *sems,
):
    i = pl.program_id(0)
    steps = pl.num_programs(0)
    at = place()
    seq, n = lax.axis_index("seq"), lax.axis_size("seq")
    L = tok.shape[0]
    bufs = (b0, b1, b2, b3)
    nc = len(CHUNKS)
    gets = []
    for (lane, width), order, buf, k in zip(CHUNKS, ORDERS, bufs, range(nc)):
        gets.append(Gather(slab.at[:, pl.ds(lane, width)], spots(buf), order, sems[2 * k : 2 * k + 2]))
    for k in range(4):
        buf = (bg_ref, bo_ref)[k % 2]
        width = buf.shape[5] // 2
        lanes = pl.ds((k // 2) * width, width)
        q = 2 * (nc + k)
        src = win_ref if k % 2 == 0 else so_ref
        gets.append(Gather(src.at[:, lanes], spots(buf, lanes), ORDERS[k], sems[q : q + 2]))
    own = []
    for k, (src, buf) in enumerate(((win_ref.at[:, pl.ds(0, DI)], bg_ref), (so_ref, bo_ref))):
        own.append(pltpu.make_async_copy(src, buf.at[at["z"], at["x"], at["y"], at["c"]], lsem.at[k]))
    halo_copy = pltpu.make_async_remote_copy(
        src_ref=tok_any.at[pl.ds(L - 16, 16)], dst_ref=halo, send_sem=hsend, recv_sem=hrecv,
        device_id={"seq": seq + 1}, device_id_type=MESH,
    )
    outs = [pltpu.make_async_copy(xhat, xhat_any, lsem.at[3]), pltpu.make_async_copy(xt, xt_any, lsem.at[4])]
    for k, (lane, width) in enumerate(CHUNKS):
        for j, (src, dst) in enumerate(((p, p_any), (wc, wc_any))):
            lanes = pl.ds(lane, width)
            outs.append(pltpu.make_async_copy(src.at[:, lanes], dst.at[:, lanes], lsem.at[5 + 2 * k + j]))

    def advance(*what):
        for k, stage in what:
            if stage > 0:
                gets[k].wait(stage - 1)
            if stage < 4:
                gets[k].start(stage)

    def project(k):
        lane, width = CHUNKS[k]
        buf = bufs[k]
        nz, rows_k = buf.shape[0], buf.shape[4]
        for z in range(nz):
            for m in range(8):
                r = z * 8 + m
                wide[r * rows_k : (r + 1) * rows_k, :width] = buf[z, m // 4, (m // 2) % 2, m % 2].astype(F32)
        wc[:, lane : lane + width] = wide[:, :width].astype(BF16)
        for r in range(L // 512):
            rows = slice(r * 512, (r + 1) * 512)
            p[rows, lane : lane + width] = dot(xhat[rows], wc[:, lane : lane + width]).astype(BF16)
        hp_ref[:, lane : lane + width] = dot(halo[...], wc[:, lane : lane + width]).astype(BF16)
        for c in outs[2 + 2 * k : 4 + 2 * k]:
            c.start()

    @pl.when(i == 0)
    def _():
        dp = lax.axis_index("dp")
        n_dp = lax.axis_size("dp")
        total = n_dp * n
        me = dp * n + seq
        load = pltpu.make_async_copy(tok_any, tok, lsem.at[2])
        load.start()
        sem = pltpu.get_barrier_semaphore()
        k_rows = slab.shape[0]
        steps_w = win_ref[:, DI + CH :]
        slab[:, :BLOCK] = jnp.concatenate([steps_w, jnp.zeros((k_rows, BLOCK - HEADS), BF16)], axis=1)
        slab[:, BLOCK:] = win_ref[:, DI : DI + CH]

        def far(o):
            r = lax.rem(me + o, total)
            return {"dp": r // n, "seq": lax.rem(r, n)}

        for o in range(1, total):
            pl.semaphore_signal(sem, inc=1, device_id=far(o), device_id_type=MESH)
        pl.semaphore_wait(sem, total - 1)
        advance((0, 0), (1, 0))

        @pl.when(seq < n - 1)
        def _():
            halo_copy.start()

        sends = []
        for o in range(1, total):
            c = pltpu.make_async_remote_copy(
                src_ref=small.at[0], dst_ref=smalls.at[me], send_sem=ssend.at[o - 1], recv_sem=srecv.at[o - 1],
                device_id=far(o), device_id_type=MESH,
            )
            c.start()
            sends.append(c)
        for c in own:
            c.start()
        smalls[me] = small[0]
        expand_row(small[1, 2:3], row_ref)
        for (lane, width), buf in zip(CHUNKS, bufs):
            buf[at["z"], at["x"], at["y"], at["c"]] = slab[:, lane : lane + width]
        conv_ref[...] = jnp.zeros_like(conv_ref)
        state[...] = jnp.zeros_like(state)
        tot_ref[...] = jnp.zeros_like(tot_ref)
        advance((0, 1), (2, 0), (1, 1), (3, 0))
        load.wait()
        for c in sends:
            c.wait()
        taps, ks, gs = CH // total, D // total, DI // total
        for r in range(total):
            conv_ref[0:5, r * taps : (r + 1) * taps] = smalls[r, 0:5, :taps]
            gain_ref[:, r * ks : (r + 1) * ks] = jnp.broadcast_to(smalls[r, 5:6, :ks], (8, ks))
            row_ref[1:2, r * gs : (r + 1) * gs] = smalls[r, 6:7, :gs]

        def norm(r, _):
            rows = pl.ds(pl.multiple_of(r * 256, 256), 256)
            h = rms_rows(tok[rows], gain_ref[0:1])
            xhat[rows] = h
            xt[:, rows] = h.T
            return _

        lax.fori_loop(0, L // 512, norm, 0)
        advance((0, 2), (1, 2), (2, 1), (4, 0), (3, 1), (5, 0), (6, 0), (7, 0))
        lax.fori_loop(L // 512, L // 256, norm, 0)
        for c in outs[:2]:
            c.start()

        @pl.when(seq == 0)
        def _():
            halo[...] = jnp.zeros_like(halo)

        @pl.when(seq > 0)
        def _():
            halo_copy.wait_recv()

        @pl.when(seq < n - 1)
        def _():
            halo_copy.wait_send()

        halo[...] = rms_rows(halo[...], gain_ref[0:1])
        for c in own:
            c.wait()
        advance((0, 3), (1, 3), (2, 2), (3, 2), (0, 4))
        project(0)
        advance((1, 4), (4, 1), (5, 1))
        project(1)
        advance((2, 3), (3, 3), (4, 2), (5, 2), (6, 1), (7, 1), (2, 4))
        project(2)
        advance((3, 4))
        project(3)
        for c in range(CH // 128):
            ext[c, 0:8] = hp_ref[:, BLOCK + c * 128 : BLOCK + (c + 1) * 128].astype(F32)[8:16]

    def tile(r0):
        for c in range(CH // 128):
            cs = slice(c * 128, (c + 1) * 128)
            ext[c, 8 : 8 + T] = p[pl.ds(r0, T), BLOCK + c * 128 : BLOCK + (c + 1) * 128].astype(F32)
            for r in range(0, T, 64):
                total = conv_ref[4:5, cs]
                for k in range(CONV):
                    total = total + ext[c, 5 + k + r : 5 + k + r + 64] * conv_ref[k : k + 1, cs]
                sg = sigmoid(total)
                v = total * sg
                act_ref[r : r + 64, cs] = v.astype(BF16)
                slope_ref[r : r + 64, cs] = (sg + v * (1.0 - sg)).astype(BF16)
        raw = p[pl.ds(r0, T), :BLOCK].astype(F32) + small[1, 0:1]
        dt_all = jnp.maximum(raw, 0.0) + jnp.log1p(jnp.exp(-jnp.abs(raw)))
        dt_ref[...] = dt_all
        sig_ref[...] = sigmoid_exact(raw)
        tril = (iota((BLOCK, BLOCK), 0) >= iota((BLOCK, BLOCK), 1)).astype(F32)
        lo = lane_lo()
        for blk in range(T // BLOCK):
            rows = slice(blk * BLOCK, (blk + 1) * BLOCK)
            dt = dt_all[rows]
            cum = dot_exact(tril, dt * small[1, 1:2]) * LOG2E
            cum_ref[rows] = cum
            end = cum[BLOCK - 1 : BLOCK]
            tot_ref[...] += jnp.broadcast_to(end, tot_ref.shape)
            wfac = jnp.exp2(end - cum) * dt
            decay = jnp.broadcast_to(jnp.exp2(end), (8, BLOCK))
            write_t = act_ref[rows, DI : DI + NSTATE].T
            for j in range(PAIRS):
                w, _, _ = expand_pair(wfac, j, lo)
                weighted[:, pair(j)] = (act_ref[rows, pair(j)].astype(F32) * w).astype(BF16)
            for q in range(PAIRS // 2):
                cs = slice(q * 256, (q + 1) * 256)
                new = dot(write_t, weighted[:, cs])
                bst_ref[blk, :, cs] = new.astype(BF16)
                d0, _, _ = expand_pair(decay, 2 * q, lo[:8])
                d1, _, _ = expand_pair(decay, 2 * q + 1, lo[:8])
                dd = jnp.concatenate([d0, d1], axis=1)[0:1]
                state[:, cs] = state[:, cs] * dd + new

    def after(step, *what):
        @pl.when(i == step)
        def _():
            advance(*what)

    after(2, (6, 2), (7, 2))
    after(4, (4, 3), (5, 3))
    after(6, (6, 3), (7, 3))

    @pl.when(i > 1)
    def _():
        ext[:, 0:8] = ext[:, T : T + 8]

    @pl.when(i > 0)
    def _():
        tile(pl.multiple_of((i - 1) * T, T))

    @pl.when(i == steps - 1)
    def _():
        leave_ref[...] = state[...]
        advance((4, 4), (5, 4), (6, 4), (7, 4))
        for c in outs:
            c.wait()


def sigmoid_exact(v):
    return 1.0 / (1.0 + jnp.exp(-v))


def second_kernel(
    T, gate_s, ng, act_ref, dt_ref, cum_ref, bst_ref, inc_ref, tok_ref, wo_ref, row_ref, et_ref,
    mixed_ref, nout_ref, ggrad_ref, mlow_ref, dcum_ref, ent_ref, egrad_ref, rg_ref, leave_ref, back_ref, cols_ref,
    ms, growth, rlow, prod, plow, state, exg, lows,
):
    i = pl.program_id(0)

    @pl.when(i == 0)
    def _():
        state[...] = inc_ref[...]
        exg[...] = jnp.ones_like(exg)
        back_ref[...] = jnp.zeros_like(back_ref)
        cols_ref[...] = jnp.zeros_like(cols_ref)

    lo = lane_lo()
    lower = iota((BLOCK, BLOCK), 0) >= iota((BLOCK, BLOCK), 1)
    nblk = T // BLOCK
    for blk in range(nblk):
        rows = slice(blk * BLOCK, (blk + 1) * BLOCK)
        cum = cum_ref[rows]
        cum_t = cum.T
        dt = dt_ref[rows]
        write = act_ref[rows, DI : DI + NSTATE]
        read = act_ref[rows, DI + NSTATE :]
        inner = jnp.where(lower, dot_nt(read, write), 0.0)
        lows[blk] = state[...].astype(BF16)
        ent_ref[blk] = lows[blk]
        for j in range(PAIRS):
            cols, a, b = expand_pair(cum, j, lo)
            ga = jnp.exp2(jnp.minimum(a - cum_t[2 * j : 2 * j + 1], 0.0)) * inner
            gb = jnp.exp2(jnp.minimum(b - cum_t[2 * j + 1 : 2 * j + 2], 0.0)) * inner
            scores = jnp.concatenate([ga.astype(BF16), gb.astype(BF16)], axis=1)
            vals = act_ref[rows, pair(j)].astype(F32)
            dtp, _, _ = expand_pair(dt, j, lo)
            vdt = (vals * dtp).astype(BF16)
            grow = jnp.exp2(cols)
            growth[rows, pair(j)] = grow
            diag = dot(scores, block_diag(vdt))
            out = dot(read, lows[blk, :, pair(j)])
            ms[rows, pair(j)] = diag + grow * out + row_ref[0:1, pair(j)] * vals
            dec = grow[BLOCK - 1 : BLOCK]
            state[:, pair(j)] = state[:, pair(j)] * dec + bst_ref[blk, :, pair(j)].astype(F32)

    sq = jnp.zeros((T, BLOCK), F32)
    ug = jnp.zeros((T, BLOCK), F32)
    for j in range(PAIRS):
        g = gate_s[:, pair(j)].astype(F32)
        gated = ms[:, pair(j)] * (g * sigmoid(g))
        sq = sq + gated * gated
        ug = ug + gated * ng[:, pair(j)].astype(F32)
    inv = lax.rsqrt(jnp.sum(sq, axis=-1, keepdims=True) * (1.0 / DI) + EPS)
    coef = jnp.sum(ug, axis=-1, keepdims=True) * (1.0 / DI) * (inv * inv * inv)
    for j in range(PAIRS):
        g = gate_s[:, pair(j)].astype(F32)
        sg = sigmoid(g)
        silu = g * sg
        m = ms[:, pair(j)]
        gated = m * silu
        nout_ref[:, pair(j)] = (gated * inv * row_ref[1:2, pair(j)]).astype(BF16)
        dg = inv * ng[:, pair(j)].astype(F32) - gated * coef
        low = (dg * silu).astype(BF16)
        mlow_ref[:, pair(j)] = low
        ggrad_ref[:, pair(j)] = (dg * m * (sg + silu * (1.0 - sg))).astype(BF16)
        vals = act_ref[:, pair(j)].astype(F32)
        lowf = low.astype(F32)
        mv = lowf * vals
        pr = lowf * m - row_ref[0:1, pair(j)] * mv
        hi = pr.astype(BF16)
        prod[:, pair(j)] = hi
        plow[:, pair(j)] = (pr - hi.astype(F32)).astype(BF16)
        rlow[:, pair(j)] = (lowf * growth[:, pair(j)]).astype(BF16)
        cols_ref[:, pair(j)] += jnp.sum(mv.reshape(T // 8, 8, BLOCK), axis=0)
    dcum_ref[...] = dot(prod[...], et_ref[...]) + dot(plow[...], et_ref[...])
    mixed_ref[...] = (tok_ref[...].astype(F32) + dot(nout_ref[...], wo_ref[...])).astype(BF16)
    for blk in range(nblk):
        rows = slice(blk * BLOCK, (blk + 1) * BLOCK)
        read_t = act_ref[rows, DI + NSTATE :].T
        for q in range(PAIRS // 2):
            cs = slice(q * 256, (q + 1) * 256)
            eg = dot(read_t, rlow[rows, cs])
            egrad_ref[blk, :, cs] = eg.astype(BF16)
            back_ref[:, cs] += eg * exg[0:1, cs]
        exg[...] = exg[...] * growth[blk * BLOCK + BLOCK - 1 : blk * BLOCK + BLOCK, :]
        rg_ref[rows] = dot_nt(rlow[rows, :], lows[blk])

    @pl.when(i == pl.num_programs(0) - 1)
    def _():
        leave_ref[...] = state[...].astype(BF16)


def third_kernel(
    T, act_ref, convin_ref, slope_ref, dt_ref, cum_ref, sig_ref, dcum_ref, mlow_ref, ent_ref, leave_ref,
    egrad_ref, rg_ref, inc_ref, row_ref, conv_ref, head_ref, et_ref, go_ref, gg_ref,
    pg_ref, cgrad_ref, hgrad_ref, tail_ref, so_ref, sg_ref,
    glast, xlast, gafter, hsend, hrecv, carry, dact, vprod, prod, plow, weighted, lows, dec, nxt, gext, *scratch,
):
    i = pl.program_id(0)
    steps = pl.num_programs(0)
    sca = Scatter(go_ref, "yx", scratch[2 : 2 + NSC], *scratch[:2])
    scb = Scatter(gg_ref, "xy", scratch[4 + NSC :], *scratch[2 + NSC : 4 + NSC])
    seq, nseq = lax.axis_index("seq"), lax.axis_size("seq")
    after = pltpu.make_async_remote_copy(
        src_ref=gext.at[:, pl.ds(0, 8)], dst_ref=gafter, send_sem=hsend, recv_sem=hrecv, device_id={"seq": seq - 1},
        device_id_type=MESH,
    )

    @pl.when(i == 0)
    def _():
        greet(place(), "zxyc", 1)
        sca.start(0)
        scb.start(0)

    for stage, when in enumerate((1, 3, 5)):
        @pl.when(i == when)
        def _():
            sca.finish(stage)
            sca.start(stage + 1)
            scb.finish(stage)
            scb.start(stage + 1)


    @pl.when(i == 0)
    def _():
        carry[...] = inc_ref[...]
        nxt[...] = leave_ref[...]
        cgrad_ref[...] = jnp.zeros_like(cgrad_ref)
        hgrad_ref[...] = jnp.zeros_like(hgrad_ref)

    lo = lane_lo()
    upper = iota((BLOCK, BLOCK), 0) <= iota((BLOCK, BLOCK), 1)
    triu = upper.astype(F32)
    last = iota((BLOCK, BLOCK), 0) == BLOCK - 1
    for blk in reversed(range(T // BLOCK)):
        rows = slice(blk * BLOCK, (blk + 1) * BLOCK)
        cum = cum_ref[rows]
        cum_t = cum.T
        dt = dt_ref[rows]
        end = cum[BLOCK - 1 : BLOCK]
        write = act_ref[rows, DI : DI + NSTATE]
        read = act_ref[rows, DI + NSTATE :]
        inner = jnp.where(upper, dot_nt(write, read), 0.0)
        lows[...] = carry[...].astype(BF16)
        acc = jnp.zeros((BLOCK, BLOCK), F32)
        for j in range(PAIRS):
            cols, a, b = expand_pair(cum, j, lo)
            ends = jnp.where(lo[:1], end[:, 2 * j : 2 * j + 1], end[:, 2 * j + 1 : 2 * j + 2])
            wexp = jnp.exp2(ends - cols)
            da = jnp.exp2(jnp.minimum(cum_t[2 * j : 2 * j + 1] - a, 0.0))
            db = jnp.exp2(jnp.minimum(cum_t[2 * j + 1 : 2 * j + 2] - b, 0.0))
            scores = jnp.concatenate([(da * inner).astype(BF16), (db * inner).astype(BF16)], axis=1)
            m = mlow_ref[rows, pair(j)]
            diag = block_diag(m)
            z = dot(scores, diag)
            vals = act_ref[rows, pair(j)].astype(F32)
            dtp, _, _ = expand_pair(dt, j, lo)
            vdt = vals * dtp
            vdtb = vdt.astype(BF16)
            wtb = (vdt * wexp).astype(BF16)
            g = dot_nt(vdtb, diag)
            acc = acc + g[:, :BLOCK] * da + g[:, BLOCK:] * db
            wg = dot(write, lows[:, pair(j)])
            pr = vdtb.astype(F32) * z + wtb.astype(F32) * wg
            z = z + wg * wexp
            dact[rows, pair(j)] = row_ref[0:1, pair(j)] * m.astype(F32) + dtp * z
            vprod[:, pair(j)] = (vals * z).astype(BF16)
            hi = pr.astype(BF16)
            prod[:, pair(j)] = hi
            plow[:, pair(j)] = (pr - hi.astype(F32)).astype(BF16)
            weighted[:, pair(j)] = wtb
            dec[0:1, pair(j)] = jnp.exp2(cols[BLOCK - 1 : BLOCK])
        low = jnp.where(upper, acc, 0.0).astype(BF16)
        dact[rows, DI : DI + NSTATE] = dot_nt(weighted[...], lows[...]) + dot(low, read)
        dact[rows, DI + NSTATE :] = rg_ref[rows] + dot(low.T, write)
        c = dot(vprod[...], et_ref[...])
        used = dot(prod[...], et_ref[...]) + dot(plow[...], et_ref[...])
        ends = jnp.sum((lows[...].astype(F32) * nxt[...].astype(F32)).reshape(16, 8, DI), axis=0)
        ends_hi = ends.astype(BF16)
        ends_lo = (ends - ends_hi.astype(F32)).astype(BF16)
        de = jnp.sum(dot(ends_hi, et_ref[...]) + dot(ends_lo, et_ref[...]), axis=0, keepdims=True)
        dc = dcum_ref[rows] - used + jnp.where(last, de, 0.0)
        da_log = dot_exact(triu, dc)
        draw = (c + da_log * head_ref[1, 1:2]) * sig_ref[rows]
        pg_ref[rows, :BLOCK] = draw.astype(BF16)
        hgrad_ref[0:8] += jnp.sum(draw.reshape(16, 8, BLOCK), axis=0)
        hgrad_ref[8:16] += jnp.sum((da_log * dt).reshape(16, 8, BLOCK), axis=0) * head_ref[1, 1:2]
        nxt[...] = ent_ref[blk]
        for q in range(PAIRS // 2):
            cs = slice(q * 256, (q + 1) * 256)
            carry[:, cs] = carry[:, cs] * dec[0:1, cs] + egrad_ref[blk, :, cs].astype(F32)

    for c in range(CH // 128):
        cs = slice(c * 128, (c + 1) * 128)
        ps = slice(BLOCK + c * 128, BLOCK + (c + 1) * 128)

        @pl.when(i == 0)
        def _():
            gext[c, T : T + 8] = jnp.zeros((8, 128), F32)
            xlast[:, cs] = convin_ref[T - 16 :, ps].astype(F32)

        @pl.when(i > 0)
        def _():
            gext[c, T : T + 8] = gext[c, 0:8]

        for r in range(0, T, 64):
            gext[c, r : r + 64] = dact[r : r + 64, cs] * slope_ref[r : r + 64, cs].astype(F32)
        sums = [jnp.zeros((8, 128), F32)] * 5
        for r in range(0, T, 64):
            x = convin_ref[r : r + 64, ps].astype(F32)
            g = gext[c, r : r + 64]
            back = g * conv_ref[3:4, cs]
            sums[4] = sums[4] + jnp.sum(g.reshape(8, 8, 128), axis=0)
            sums[3] = sums[3] + jnp.sum((g * x).reshape(8, 8, 128), axis=0)
            for k in range(CONV - 1):
                gk = gext[c, 3 - k + r : 3 - k + r + 64]
                back = back + gk * conv_ref[k : k + 1, cs]
                sums[k] = sums[k] + jnp.sum((gk * x).reshape(8, 8, 128), axis=0)
            pg_ref[r : r + 64, ps] = back.astype(BF16)
            if r + 64 == T:
                @pl.when(i == 0)
                def _():
                    glast[:, cs] = back[48:]
        for k in range(5):
            cgrad_ref[8 * k : 8 * k + 8, cs] += sums[k]

    @pl.when(i == steps - 1)
    def _():
        @pl.when(seq > 0)
        def _():
            after.start()

        so_ref[...] = sca.result()
        sg_ref[...] = scb.result()

        @pl.when(seq == nseq - 1)
        def _():
            gafter[...] = jnp.zeros_like(gafter)

        @pl.when(seq < nseq - 1)
        def _():
            after.wait_recv()

        row16, row8 = iota((16, 128), 0), iota((8, 128), 0)
        for c in range(CH // 128):
            cs = slice(c * 128, (c + 1) * 128)
            ps = slice(BLOCK + c * 128, BLOCK + (c + 1) * 128)
            tail = glast[:, cs]
            for j in range(CONV - 1):
                for k in range(j + 1):
                    g = gafter[c, j - k : j - k + 1]
                    tail = tail + jnp.where(row16 == 13 + j, g * conv_ref[k : k + 1, cs], 0.0)
                    cgrad_ref[8 * k : 8 * k + 8, cs] += jnp.where(row8 == 0, g * xlast[13 + j : 14 + j, cs], 0.0)
            tail_ref[:, ps] = tail.astype(BF16)
        tail_ref[:, :BLOCK] = jnp.zeros((16, BLOCK), BF16)

        @pl.when(seq > 0)
        def _():
            after.wait_send()


def once(shape):
    return pl.BlockSpec(shape, lambda i: (0,) * len(shape), pipeline_mode=pl.Buffered(1))


def full(shape):
    return pl.BlockSpec(shape, lambda i: (0,) * len(shape))


def params(collective_id=None):
    return pltpu.CompilerParams(
        dimension_semantics=("arbitrary",), vmem_limit_bytes=VMEM_LIMIT, collective_id=collective_id,
        has_side_effects=collective_id is not None,
    )


def head_columns():
    et = np.zeros((DI, BLOCK), np.float32)
    et[np.arange(DI), np.arange(DI) // HEADDIM] = 1.0
    return et


def sds(shape, dtype):
    return jax.ShapeDtypeStruct(shape, dtype)


def first_pass(w_in, small, tok, slab_o, T=256):
    L = tok.shape[0]
    nb, per = L // BLOCK, T // BLOCK
    n = sizes()
    k_rows = w_in.shape[0]
    total = lax.axis_size("dp") * lax.axis_size("seq")
    row = lambda w: pl.BlockSpec((T, w), lambda i: (jnp.maximum(i - 1, 0), 0))
    dims = (n["z"], n["x"], n["y"], n["c"])
    sems = []
    for _ in range(len(CHUNKS) + 4):
        sems += gather_sems()
    return pl.pallas_call(
        functools.partial(first_kernel, T),
        grid=(1 + L // T,),
        in_specs=[once(w_in.shape), once((2, 8, BLOCK)), ANY, ANY],
        out_specs=[
            ANY, ANY, ANY, ANY, full((16, WC)), full((8, CH)), full((8, D)), full((8, DI)),
            row(CH), row(CH), row(BLOCK), row(BLOCK), row(BLOCK),
            pl.BlockSpec((per, NSTATE, DI), lambda i: (jnp.maximum(i - 1, 0), 0, 0)), full((NSTATE, DI)),
            full((8, BLOCK)), ANY, ANY,
        ],
        out_shape=[
            sds((L, D), BF16), sds((D, L), BF16), sds((D, WC), BF16), sds((L, WC), BF16), sds((16, WC), BF16),
            sds((8, CH), F32), sds((8, D), F32), sds((8, DI), F32),
            sds((L, CH), BF16), sds((L, CH), BF16), sds((L, BLOCK), F32), sds((L, BLOCK), F32), sds((L, BLOCK), F32),
            sds((nb, NSTATE, DI), BF16), sds((NSTATE, DI), F32), sds((8, BLOCK), F32),
            sds(dims + (k_rows, DI), BF16), sds(dims + slab_o.shape, BF16),
        ],
        scratch_shapes=[
            pltpu.VMEM((k_rows, WC), BF16), pltpu.VMEM((L, D), BF16), pltpu.VMEM((16, D), BF16), pltpu.VMEM((L, D), BF16), pltpu.VMEM((D, L), BF16),
            pltpu.VMEM((D, WC), BF16), pltpu.VMEM((D, 512), F32), pltpu.VMEM((L, WC), BF16),
            pltpu.VMEM((total, 8, BLOCK), F32),
        ] + [pltpu.VMEM(dims + (k_rows, w), BF16) for _, w in CHUNKS] + [
            pltpu.VMEM((CH // 128, T + 8, 128), F32), pltpu.VMEM((NSTATE, DI), F32), pltpu.VMEM((BLOCK, DI), BF16),
            pltpu.SemaphoreType.DMA((5 + 2 * len(CHUNKS),)), pltpu.SemaphoreType.DMA(()), pltpu.SemaphoreType.DMA(()),
            pltpu.SemaphoreType.DMA((total - 1,)), pltpu.SemaphoreType.DMA((total - 1,)),
        ] + sems,
        compiler_params=params(collective_id=1),
        name="first_pass",
    )(w_in, small, tok, slab_o)


def second_pass(gate, ng, act, dt, cum, bst, inc, tok, wo, rows, et, T=256):
    L = tok.shape[0]
    nb, per = L // BLOCK, T // BLOCK
    row = lambda w: pl.BlockSpec((T, w), lambda i: (i, 0))
    blk = pl.BlockSpec((per, NSTATE, DI), lambda i: (i, 0, 0))
    return pl.pallas_call(
        functools.partial(second_kernel, T),
        grid=(L // T,),
        in_specs=[
            row(DI), row(DI), row(CH), row(BLOCK), row(BLOCK), blk, full((NSTATE, DI)), row(D), full((DI, D)), full((8, DI)), full((DI, BLOCK)),
        ],
        out_specs=[
            row(D), row(DI), row(DI), row(DI), row(BLOCK), blk, blk, row(BLOCK), full((NSTATE, DI)),
            full((NSTATE, DI)), full((8, DI)),
        ],
        out_shape=[
            sds((L, D), BF16), sds((L, DI), BF16), sds((L, DI), BF16), sds((L, DI), BF16), sds((L, BLOCK), F32),
            sds((nb, NSTATE, DI), BF16), sds((nb, NSTATE, DI), BF16), sds((L, BLOCK), F32), sds((NSTATE, DI), BF16),
            sds((NSTATE, DI), F32), sds((8, DI), F32),
        ],
        scratch_shapes=[
            pltpu.VMEM((T, DI), F32), pltpu.VMEM((T, DI), F32),
            pltpu.VMEM((T, DI), BF16), pltpu.VMEM((T, DI), BF16), pltpu.VMEM((T, DI), BF16), pltpu.VMEM((NSTATE, DI), F32),
            pltpu.VMEM((8, DI), F32), pltpu.VMEM((per, NSTATE, DI), BF16),
        ],
        compiler_params=params(),
        name="second_pass",
    )(gate, ng, act, dt, cum, bst, inc, tok, wo, rows, et)


def third_pass(
    act, convin, slope, dt, cum, sig, dcum, mlow, ent, leave, egrad, rg, inc, rows, conv, head, et, go, gg, T=256
):
    L = act.shape[0]
    m = sizes()
    dims = (m["z"], m["x"], m["y"], m["c"])
    total = m["z"] * m["y"] * 4
    ro, rg_rows = DI // total, D // total
    go = go.reshape(dims + (ro, D))
    gg = gg.reshape(dims + (rg_rows, DI))
    n, per = L // T, T // BLOCK
    row = lambda w: pl.BlockSpec((T, w), lambda i: (n - 1 - i, 0))
    blk = pl.BlockSpec((per, NSTATE, DI), lambda i: (n - 1 - i, 0, 0))
    return pl.pallas_call(
        functools.partial(third_kernel, T),
        grid=(n,),
        in_specs=[
            row(CH), row(WC), row(CH), row(BLOCK), row(BLOCK), row(BLOCK), row(BLOCK), row(DI), blk,
            full((NSTATE, DI)), blk, row(BLOCK), full((NSTATE, DI)), full((8, DI)), full((8, CH)), full((2, 8, BLOCK)),
            full((DI, BLOCK)), ANY, ANY,
        ],
        out_specs=[
            row(WC), full((40, CH)), full((16, BLOCK)), full((16, WC)), full((ro, D)), full((rg_rows, DI)),
        ],
        out_shape=[
            sds((L, WC), BF16), sds((40, CH), F32), sds((16, BLOCK), F32), sds((16, WC), BF16), sds((ro, D), F32),
            sds((rg_rows, DI), F32),
        ],
        scratch_shapes=[
            pltpu.VMEM((16, CH), F32), pltpu.VMEM((16, CH), F32), pltpu.VMEM((CH // 128, 8, 128), F32),
            pltpu.SemaphoreType.DMA(()), pltpu.SemaphoreType.DMA(()),
            pltpu.VMEM((NSTATE, DI), F32), pltpu.VMEM((T, CH), F32), pltpu.VMEM((BLOCK, DI), BF16), pltpu.VMEM((BLOCK, DI), BF16), pltpu.VMEM((BLOCK, DI), BF16),
            pltpu.VMEM((BLOCK, DI), BF16), pltpu.VMEM((NSTATE, DI), BF16), pltpu.VMEM((8, DI), F32),
            pltpu.VMEM((NSTATE, DI), BF16), pltpu.VMEM((CH // 128, T + 8, 128), F32),
        ] + own_scratch(ro, D) + scatter_scratch(ro, D) + own_scratch(rg_rows, DI) + scatter_scratch(rg_rows, DI),
        compiler_params=params(collective_id=4),
        name="third_pass",
    )(act, convin, slope, dt, cum, sig, dcum, mlow, ent, leave, egrad, rg, inc, rows, conv, head, et, go, gg)


def on_device(
    tokens, cotangent, norm_gain, in_weight, conv_weight, conv_bias, step_bias, decay_log, skip_gain, gate_gain,
    out_weight,
):
    tok, cot = tokens[0], cotangent[0]
    L = tok.shape[0]
    k_rows, c_rows = in_weight.shape[0], conv_weight.shape[0]
    total = D // k_rows
    lanes = lambda x: jnp.pad(x, ((0, 0),) * (x.ndim - 1) + ((0, BLOCK - x.shape[-1]),))

    def put(x, row):
        x = x.astype(F32)
        return jnp.pad(x, ((row, 16 - row - x.shape[0]), (0, BLOCK - x.shape[1])))

    own = put(conv_weight.T, 0) + put(conv_bias[None], 4) + put(norm_gain[None], 5) + put(gate_gain[None], 6)
    own = own + put(step_bias[None], 8) + put(-jnp.exp(decay_log)[None], 9) + put(skip_gain[None], 10)
    own = own.reshape(2, 8, BLOCK)
    et = jnp.asarray(head_columns(), BF16)

    (xhat, xt, wc, p, hp, conv, gain, rows, act, slope, dt, cum, sig, bst, leave, tot, buf_g, buf_o) = first_pass(
        in_weight, own, tok, out_weight
    )
    wg, wo = buf_g.reshape(D, DI), buf_o.reshape(DI, D)
    gate, ng, inc = gate_pass(xhat, wg, cot, wo, rows, leave, tot)
    mixed, nout, ggrad, mlow, dcum, ent, egrad, rg, leave2, back, cols = second_pass(
        gate, ng, act, dt, cum, bst, inc, tok, wo, rows, et
    )
    g_out, g_gate, later = grads_pass(nout, cot, xt, ggrad, back, tot)
    pg, cgrad, hgrad, tail, out_raw, gate_cols = third_pass(
        act, p, slope, dt, cum, sig, dcum, mlow, ent, leave2, egrad, rg, later, rows, conv, own, et, g_out, g_gate
    )
    cg = cgrad.reshape(5, 8, CH).sum(axis=1)
    hg = hgrad.reshape(2, 8, BLOCK).sum(axis=1)[:, :HEADS]
    sums = jnp.concatenate([hg[0], hg[1], cols.reshape(8, HEADS, HEADDIM).sum(axis=(0, 2))])
    small = jnp.concatenate(
        [
            lanes(jnp.swapaxes(cg.reshape(5, total, c_rows), 0, 1)), jnp.zeros((total, 2, BLOCK), F32),
            jnp.broadcast_to(lanes(sums[None, None]), (total, 1, BLOCK)),
        ],
        axis=1,
    )
    tgrad, conv_cols, sums = last_pass(xt, pg, tail, ggrad, tok, cot, wg, wc, gain, small)
    in_grad, ngain_grad, ggain_grad, taps, bias, step, decay, skip, out_grad, tgrad = finish_pass(
        gate_cols, conv_cols, out_raw, sums, in_weight, out_weight, norm_gain.astype(F32), gate_gain.astype(F32), tgrad,
        c_rows,
    )
    return (
        mixed[None], tgrad[None], ngain_grad, in_grad, taps, bias, step, decay, skip, ggain_grad, out_grad,
    )


def solution(mesh):
    both = ("dp", "seq")
    vec, mat, tok, rep = P(both), P(both, None), P("dp", "seq", None), P()
    return jax.shard_map(
        on_device,
        mesh=mesh,
        in_specs=(tok, tok, vec, mat, mat, vec, rep, rep, rep, vec, mat),
        out_specs=(tok, tok, vec, mat, mat, vec, rep, rep, rep, vec, mat),
        check_vma=False,
    )
```

profile of v0, /device:TPU:0, one launch (start us, length us, event | category | flops | bytes accessed | tf_op | source)
XLA Modules:
  0.0 276.0 jit_solution(15822516184882073885)
XLA Ops:
  0.6 1.2 fusion.1
  1.8 1.2 fusion.2
  3.0 0.7 negate_bitcast_fusion
  3.7 1.3 add_bitcast_fusion.small.head_ref
  5.0 70.8 %first_pass.1 = (bf16[2048,768]{1,0:T(8,128)(2,1)}, bf16[768,2048]{1,0:T(8,128)(2,1)}, bf16[768,1920]{1,0:T(8,128)(2,1)}, bf16[2048,1920]{1,0:T(8,128)(2,1)}, bf...) custom-call(bf16[24,3352]{1,0:T(8,128)(2,1)} %w_ref.1, ...), custom_call_target="tpu_custom_call" | custom-call | tf_op jit(solution)/shard_map/first_pass/pallas_call | solution.py:1164
  75.9 16.2 %gate_pass.1 = (bf16[2048,1536]{1,0:T(8,128)(2,1)}, bf16[2048,1536]{1,0:T(8,128)(2,1)}, f32[128,1536]{1,0:T(8,128)}) custom-call(bf16[2048,768]{1,0:T(8,128)(2,1)} %get-tuple-element.64.normed_ref, bf16[768,1536]{1,0:T(8,128)(2,1)} %bitcast.41, bf16[2048,768]{1,0:T(8,128)(2,1)} %bitcast.38, bf16[1536,768]{1,0:T(8,128)(2,1)} %bitcast.43, ...), custom_call_target="tpu_custom_call" | custom-call | tf_op jit(solution)/shard_map/gate_pass/pallas_call | solution.py:386
  92.1 52.9 %second_pass.1 = (bf16[2048,768]{1,0:T(8,128)(2,1)}, bf16[2048,1536]{1,0:T(8,128)(2,1)}, bf16[2048,1536]{1,0:T(8,128)(2,1)}, bf16[2048,1536]{1,0:T(8,128)(2,1)},...) custom-call(bf16[2048,1536]{1,0:T(8,128)(2,1)} %get-tuple-element.70, ...), custom_call_target="tpu_custom_call" | custom-call | tf_op jit(solution)/shard_map/second_pass/pallas_call | solution.py:1200
  145.0 18.0 %grads_pass.1 = (bf16[1536,768]{1,0:T(8,128)(2,1)}, bf16[768,1536]{1,0:T(8,128)(2,1)}, f32[128,1536]{1,0:T(8,128)}) custom-call(bf16[2048,1536]{1,0:T(8,128)(2,1)} %get-tuple-element.87.nout_ref, bf16[2048,768]{1,0:T(8,128)(2,1)} %bitcast.39, bf16[768,2048]{1,0:T(8,128)(2,1)} %get-tuple-element.88.xt_ref.xt_any, ...), custom_call_target="tpu_custom_call" | custom-call | tf_op jit(solution)/shard_map/grads_pass/pallas_call | solution.py:426
  163.0 0.0 copy-start
  163.0 63.5 %third_pass.1 = (bf16[2048,1920]{1,0:T(8,128)(2,1)}, f32[40,1792]{1,0:T(8,128)}, f32[16,128]{1,0:T(8,128)}, bf16[16,1920]{1,0:T(8,128)(2,1)}, f32[48,768]{1,0:T(8,128)}, /*index=5*/f32[24,1536]{1,0:T(8,128)}) custom-call(bf16[2048,1792]{1,0:T(8,128)(2,1)} %get-tuple-element.72.act_ref, bf16[2048,1920]{1,0:T(8,128)(2,1)} %get-tuple-element.78.convin_ref, ...), custom_call_target="tpu_custom_call" | custom-call | tf_op jit(solution)/shard_map/third_pass/pallas_call | solution.py:1238
  226.5 0.7 bitcast_reduce_fusion.1
  227.3 0.0 copy-done
  227.3 0.1 reduce_sum.37
  227.4 0.1 reduce_sum.38
  227.5 0.1 maximum_bitcast_fusion
  227.6 1.0 bitcast_reduce_fusion
  228.6 0.1 reshape.61
  228.7 0.1 copy.29
  228.8 0.1 pad.54.clone
  228.9 0.7 fusion.small_ref
  229.6 40.0 %last_pass.1 = (bf16[2048,768]{1,0:T(8,128)(2,1)}, f32[24,1920]{1,0:T(8,128)}, f32[8,128]{1,0:T(8,128)}) custom-call(bf16[768,2048]{1,0:T(8,128)(2,1)} %get-tuple-element.88.xt_ref.xt_any, bf16[2048,1920]{1,0:T(8,128)(2,1)} %get-tuple-element.96.pg_any, bf16[768,1536]{1,0:T(8,128)(2,1)} %bitcast.42, bf16[768,1920]{1,0:T(8,128)(2,1)} %get-tuple-element.97.wc_any, ...), custom_call_target="tpu_custom_call" | custom-call | tf_op jit(solution)/shard_map/last_pass/pallas_call | solution.py:569
  269.7 4.9 %finish_pass.1 = (f32[24,3352]{1,0:T(8,128)}, f32[24]{0:T(128)}, f32[48]{0:T(128)}, f32[56,4]{1,0:T(8,128)}, f32[56]{0:T(128)}, /*index=5*/f32[24]{0:T(128)}, f3...) custom-call(f32[24,1536]{1,0:T(8,128)} %get-tuple-element.95.gate_ref, ...), custom_call_target="tpu_custom_call" | custom-call | tf_op jit(solution)/shard_map/finish_pass/pallas_call | solution.py:632
  274.6 1.4 copy.27
  (5 shorter events, 0.0 us)
Async XLA Ops:
  163.0 64.3 %copy-start = (f32[8,1536]{1,0:T(8,128)S(1)}, f32[8,1536]{1,0:T(8,128)}, u32[]{:S(2)}) copy-start(f32[8,1536]{1,0:T(8,128)} %get-tuple-element.102) | copy-start | bytes 147460
where the time goes:
time: 276 us
  Pallas kernels  266 us (96%)
  other arithmetic  7.1 us (3%)
    pallas_call x1, Pallas kernels, first_pass(): pl.pallas_call(functools.partial(first_kernel, T), grid=(1 + L // T,), in...  70.8 us
    pallas_call x1, Pallas kernels, third_pass(): pl.pallas_call(functools.partial(third_kernel, T), grid=(n,), in_specs=[r...  63.5 us
    pallas_call x1, Pallas kernels, second_pass(): pl.pallas_call(functools.partial(second_kernel, T), grid=(L // T,), in_sp...  52.9 us
    pallas_call x1, Pallas kernels, last_pass(): pl.pallas_call(functools.partial(last_kernel, T), grid=(nc + L // T,), in...  40 us
    pallas_call x1, Pallas kernels, grads_pass(): pl.pallas_call(grads_kernel, grid=(6,), in_specs=[col(256), full((L, D)),...  18 us
    pallas_call x1, Pallas kernels, gate_pass(): pl.pallas_call(gate_kernel, grid=(L // T,), in_specs=[row(D), full((D, DI...  16.2 us

commit v1 on v0

--- a/solution.py
+++ b/solution.py
@@ -588,7 +588,7 @@
 
 
 def finish_kernel(
-    gate_ref, conv_ref, out_ref, sums_ref, w_ref, wo_ref, gain_ref, ggain_ref, tgrad_ref,
+    gate_ref, conv_ref, out_ref, sums_ref, w_ref, wo_ref, own_ref, tgrad_ref,
     in_grad, ngain, ggain, taps, bias, step, decay, skip, out_grad, tgrad_out,
 ):
     tgrad_out[...] = tgrad_ref[...]
@@ -596,39 +596,39 @@
     @pl.when(pl.program_id(0) == 0)
     def _():
         finish_small(
-            gate_ref, conv_ref, out_ref, sums_ref, w_ref, wo_ref, gain_ref, ggain_ref, in_grad, ngain, ggain, taps, bias,
+            gate_ref, conv_ref, out_ref, sums_ref, w_ref, wo_ref, own_ref, in_grad, ngain, ggain, taps, bias,
             step, decay, skip, out_grad,
         )
 
 
 def finish_small(
-    gate_ref, conv_ref, out_ref, sums_ref, w_ref, wo_ref, gain_ref, ggain_ref,
+    gate_ref, conv_ref, out_ref, sums_ref, w_ref, wo_ref, own_ref,
     in_grad, ngain, ggain, taps, bias, step, decay, skip, out_grad,
 ):
     conv = conv_ref[...]
     raw = jnp.concatenate([gate_ref[...], conv[:, BLOCK:], conv[:, :HEADS]], axis=1)
     in_grad[...] = raw
-    ngain[...] = jnp.sum(raw * w_ref[...].astype(F32), axis=1) / gain_ref[...]
+    ngain[...] = jnp.sum(raw * w_ref[...].astype(F32), axis=1) / own_ref[0, 5, : ngain.shape[0]]
     o = out_ref[...]
     out_grad[...] = o
-    ggain[...] = jnp.sum(o * wo_ref[...].astype(F32), axis=1) / ggain_ref[...]
+    ggain[...] = jnp.sum(o * wo_ref[...].astype(F32), axis=1) / own_ref[0, 6, : ggain.shape[0]]
     s = sums_ref[...]
     n = bias.shape[0]
-    taps[...] = s.T[:n, :CONV]
+    taps[...] = s[:CONV, :n]
     bias[...] = s[4, :n]
     step[...] = s[7, :HEADS]
     decay[...] = s[7, HEADS : 2 * HEADS]
     skip[...] = s[7, 2 * HEADS : 3 * HEADS]
 
 
-def finish_pass(gate_cols, conv_cols, out_raw, sums, w, wo, gain, ggain, tgrad, channels):
+def finish_pass(gate_cols, conv_cols, out_raw, sums, w, wo, own, tgrad, channels):
     vec = lambda n: sds((n,), F32)
     rows = pl.BlockSpec((512, D), lambda i: (i, 0))
     small = [
-        sds(w.shape, F32), vec(w.shape[0]), vec(wo.shape[0]), sds((channels, CONV), F32),
+        sds(w.shape, F32), vec(w.shape[0]), vec(wo.shape[0]), sds((CONV, channels), F32),
         vec(channels), vec(HEADS), vec(HEADS), vec(HEADS), sds(out_raw.shape, F32),
     ]
-    ins = (gate_cols, conv_cols, out_raw, sums, w, wo, gain, ggain)
+    ins = (gate_cols, conv_cols, out_raw, sums, w, wo, own)
     return pl.pallas_call(
         finish_kernel,
         grid=(tgrad.shape[0] // 512,),
@@ -818,7 +818,7 @@
         for blk in range(T // BLOCK):
             rows = slice(blk * BLOCK, (blk + 1) * BLOCK)
             dt = dt_all[rows]
-            cum = dot_exact(tril, dt * small[1, 1:2]) * LOG2E
+            cum = dot_exact(tril, dt * -jnp.exp(small[1, 1:2])) * LOG2E
             cum_ref[rows] = cum
             end = cum[BLOCK - 1 : BLOCK]
             tot_ref[...] += jnp.broadcast_to(end, tot_ref.shape)
@@ -904,7 +904,9 @@
             grow = jnp.exp2(cols)
             growth[rows, pair(j)] = grow
             diag = dot(scores, block_diag(vdt))
-            out = dot(read, lows[blk, :, pair(j)])
+            if j % 2 == 0:
+                outs = dot(read, lows[blk, :, j * BLOCK : (j + 2) * BLOCK])
+            out = outs[:, (j % 2) * BLOCK : (j % 2 + 1) * BLOCK]
             ms[rows, pair(j)] = diag + grow * out + row_ref[0:1, pair(j)] * vals
             dec = grow[BLOCK - 1 : BLOCK]
             state[:, pair(j)] = state[:, pair(j)] * dec + bst_ref[blk, :, pair(j)].astype(F32)
@@ -958,9 +960,9 @@
 
 def third_kernel(
     T, act_ref, convin_ref, slope_ref, dt_ref, cum_ref, sig_ref, dcum_ref, mlow_ref, ent_ref, leave_ref,
-    egrad_ref, rg_ref, inc_ref, row_ref, conv_ref, head_ref, et_ref, go_ref, gg_ref,
-    pg_ref, cgrad_ref, hgrad_ref, tail_ref, so_ref, sg_ref,
-    glast, xlast, gafter, hsend, hrecv, carry, dact, vprod, prod, plow, weighted, lows, dec, nxt, gext, *scratch,
+    egrad_ref, rg_ref, inc_ref, row_ref, conv_ref, head_ref, et_ref, cols_ref, go_ref, gg_ref,
+    pg_ref, small_ref, tail_ref, so_ref, sg_ref,
+    cgrad_ref, hgrad_ref, sums8, glast, xlast, gafter, hsend, hrecv, carry, dact, vprod, prod, plow, weighted, lows, dec, nxt, gext, *scratch,
 ):
     i = pl.program_id(0)
     steps = pl.num_programs(0)
@@ -1026,7 +1028,9 @@
             wtb = (vdt * wexp).astype(BF16)
             g = dot_nt(vdtb, diag)
             acc = acc + g[:, :BLOCK] * da + g[:, BLOCK:] * db
-            wg = dot(write, lows[:, pair(j)])
+            if j % 2 == 0:
+                wgs = dot(write, lows[:, j * BLOCK : (j + 2) * BLOCK])
+            wg = wgs[:, (j % 2) * BLOCK : (j % 2 + 1) * BLOCK]
             pr = vdtb.astype(F32) * z + wtb.astype(F32) * wg
             z = z + wg * wexp
             dact[rows, pair(j)] = row_ref[0:1, pair(j)] * m.astype(F32) + dtp * z
@@ -1047,10 +1051,11 @@
         de = jnp.sum(dot(ends_hi, et_ref[...]) + dot(ends_lo, et_ref[...]), axis=0, keepdims=True)
         dc = dcum_ref[rows] - used + jnp.where(last, de, 0.0)
         da_log = dot_exact(triu, dc)
-        draw = (c + da_log * head_ref[1, 1:2]) * sig_ref[rows]
+        decay = -jnp.exp(head_ref[1, 1:2])
+        draw = (c + da_log * decay) * sig_ref[rows]
         pg_ref[rows, :BLOCK] = draw.astype(BF16)
         hgrad_ref[0:8] += jnp.sum(draw.reshape(16, 8, BLOCK), axis=0)
-        hgrad_ref[8:16] += jnp.sum((da_log * dt).reshape(16, 8, BLOCK), axis=0) * head_ref[1, 1:2]
+        hgrad_ref[8:16] += jnp.sum((da_log * dt).reshape(16, 8, BLOCK), axis=0) * decay
         nxt[...] = ent_ref[blk]
         for q in range(PAIRS // 2):
             cs = slice(q * 256, (q + 1) * 256)
@@ -1119,6 +1124,22 @@
                     cgrad_ref[8 * k : 8 * k + 8, cs] += jnp.where(row8 == 0, g * xlast[13 + j : 14 + j, cs], 0.0)
             tail_ref[:, ps] = tail.astype(BF16)
         tail_ref[:, :BLOCK] = jnp.zeros((16, BLOCK), BF16)
+        for k in range(5):
+            sums8[k : k + 1] = jnp.sum(cgrad_ref[8 * k : 8 * k + 8], axis=0, keepdims=True)
+        steps8 = jnp.broadcast_to(jnp.sum(hgrad_ref[0:8], axis=0, keepdims=True), (8, BLOCK))
+        decay8 = jnp.broadcast_to(jnp.sum(hgrad_ref[8:16], axis=0, keepdims=True), (8, BLOCK))
+        high = cols_ref[...].astype(BF16)
+        low8 = (cols_ref[...] - high.astype(F32)).astype(BF16)
+        skip8 = jnp.sum(dot(high, et_ref[...]) + dot(low8, et_ref[...]), axis=0, keepdims=True)
+        skip8 = jnp.broadcast_to(skip8, (8, BLOCK))
+        lane = iota((8, BLOCK), 1)
+        heads = jnp.where(lane < HEADS, steps8, pltpu.roll(decay8, HEADS, 1))
+        heads = jnp.where(lane < 2 * HEADS, heads, pltpu.roll(skip8, 2 * HEADS, 1))
+        heads = jnp.where((iota((8, BLOCK), 0) == 7) & (lane < 3 * HEADS), heads, 0.0)
+        take = CH // small_ref.shape[0]
+        for r in range(small_ref.shape[0]):
+            small_ref[r] = heads
+            small_ref[r, 0:5, :take] = sums8[0:5, r * take : (r + 1) * take]
 
         @pl.when(seq > 0)
         def _():
@@ -1223,7 +1244,7 @@
 
 
 def third_pass(
-    act, convin, slope, dt, cum, sig, dcum, mlow, ent, leave, egrad, rg, inc, rows, conv, head, et, go, gg, T=256
+    act, convin, slope, dt, cum, sig, dcum, mlow, ent, leave, egrad, rg, inc, rows, conv, head, et, cols, go, gg, T=256
 ):
     L = act.shape[0]
     m = sizes()
@@ -1241,16 +1262,17 @@
         in_specs=[
             row(CH), row(WC), row(CH), row(BLOCK), row(BLOCK), row(BLOCK), row(BLOCK), row(DI), blk,
             full((NSTATE, DI)), blk, row(BLOCK), full((NSTATE, DI)), full((8, DI)), full((8, CH)), full((2, 8, BLOCK)),
-            full((DI, BLOCK)), ANY, ANY,
+            full((DI, BLOCK)), full((8, DI)), ANY, ANY,
         ],
         out_specs=[
-            row(WC), full((40, CH)), full((16, BLOCK)), full((16, WC)), full((ro, D)), full((rg_rows, DI)),
+            row(WC), full((total, 8, BLOCK)), full((16, WC)), full((ro, D)), full((rg_rows, DI)),
         ],
         out_shape=[
-            sds((L, WC), BF16), sds((40, CH), F32), sds((16, BLOCK), F32), sds((16, WC), BF16), sds((ro, D), F32),
+            sds((L, WC), BF16), sds((total, 8, BLOCK), F32), sds((16, WC), BF16), sds((ro, D), F32),
             sds((rg_rows, DI), F32),
         ],
         scratch_shapes=[
+            pltpu.VMEM((40, CH), F32), pltpu.VMEM((16, BLOCK), F32), pltpu.VMEM((8, CH), F32),
             pltpu.VMEM((16, CH), F32), pltpu.VMEM((16, CH), F32), pltpu.VMEM((CH // 128, 8, 128), F32),
             pltpu.SemaphoreType.DMA(()), pltpu.SemaphoreType.DMA(()),
             pltpu.VMEM((NSTATE, DI), F32), pltpu.VMEM((T, CH), F32), pltpu.VMEM((BLOCK, DI), BF16), pltpu.VMEM((BLOCK, DI), BF16), pltpu.VMEM((BLOCK, DI), BF16),
@@ -1259,7 +1281,7 @@
         ] + own_scratch(ro, D) + scatter_scratch(ro, D) + own_scratch(rg_rows, DI) + scatter_scratch(rg_rows, DI),
         compiler_params=params(collective_id=4),
         name="third_pass",
-    )(act, convin, slope, dt, cum, sig, dcum, mlow, ent, leave, egrad, rg, inc, rows, conv, head, et, go, gg)
+    )(act, convin, slope, dt, cum, sig, dcum, mlow, ent, leave, egrad, rg, inc, rows, conv, head, et, cols, go, gg)
 
 
 def on_device(
@@ -1277,7 +1299,7 @@
         return jnp.pad(x, ((row, 16 - row - x.shape[0]), (0, BLOCK - x.shape[1])))
 
     own = put(conv_weight.T, 0) + put(conv_bias[None], 4) + put(norm_gain[None], 5) + put(gate_gain[None], 6)
-    own = own + put(step_bias[None], 8) + put(-jnp.exp(decay_log)[None], 9) + put(skip_gain[None], 10)
+    own = own + put(step_bias[None], 8) + put(decay_log[None], 9) + put(skip_gain[None], 10)
     own = own.reshape(2, 8, BLOCK)
     et = jnp.asarray(head_columns(), BF16)
 
@@ -1290,26 +1312,16 @@
         gate, ng, act, dt, cum, bst, inc, tok, wo, rows, et
     )
     g_out, g_gate, later = grads_pass(nout, cot, xt, ggrad, back, tot)
-    pg, cgrad, hgrad, tail, out_raw, gate_cols = third_pass(
-        act, p, slope, dt, cum, sig, dcum, mlow, ent, leave2, egrad, rg, later, rows, conv, own, et, g_out, g_gate
-    )
-    cg = cgrad.reshape(5, 8, CH).sum(axis=1)
-    hg = hgrad.reshape(2, 8, BLOCK).sum(axis=1)[:, :HEADS]
-    sums = jnp.concatenate([hg[0], hg[1], cols.reshape(8, HEADS, HEADDIM).sum(axis=(0, 2))])
-    small = jnp.concatenate(
-        [
-            lanes(jnp.swapaxes(cg.reshape(5, total, c_rows), 0, 1)), jnp.zeros((total, 2, BLOCK), F32),
-            jnp.broadcast_to(lanes(sums[None, None]), (total, 1, BLOCK)),
-        ],
-        axis=1,
+    pg, small, tail, out_raw, gate_cols = third_pass(
+        act, p, slope, dt, cum, sig, dcum, mlow, ent, leave2, egrad, rg, later, rows, conv, own, et, cols, g_out,
+        g_gate,
     )
     tgrad, conv_cols, sums = last_pass(xt, pg, tail, ggrad, tok, cot, wg, wc, gain, small)
     in_grad, ngain_grad, ggain_grad, taps, bias, step, decay, skip, out_grad, tgrad = finish_pass(
-        gate_cols, conv_cols, out_raw, sums, in_weight, out_weight, norm_gain.astype(F32), gate_gain.astype(F32), tgrad,
-        c_rows,
+        gate_cols, conv_cols, out_raw, sums, in_weight, out_weight, own, tgrad, c_rows
     )
     return (
-        mixed[None], tgrad[None], ngain_grad, in_grad, taps, bias, step, decay, skip, ggain_grad, out_grad,
+        mixed[None], tgrad[None], ngain_grad, in_grad, taps.T, bias, step, decay, skip, ggain_grad, out_grad,
     )
 
 

time: 276 us -> 269 us (0.975)
  other arithmetic: 7.1 us -> 1.38 us
where the time goes in v1:
time: 269 us
  Pallas kernels  267 us (99%)
    pallas_call x1, Pallas kernels, first_pass(): pl.pallas_call(functools.partial(first_kernel, T), grid=(1 + L // T,), in...  70.8 us
    pallas_call x1, Pallas kernels, third_pass(): pl.pallas_call(functools.partial(third_kernel, T), grid=(n,), in_specs=[r...  63.9 us
    pallas_call x1, Pallas kernels, second_pass(): pl.pallas_call(functools.partial(second_kernel, T), grid=(L // T,), in_sp...  52.5 us
    pallas_call x1, Pallas kernels, last_pass(): pl.pallas_call(functools.partial(last_kernel, T), grid=(nc + L // T,), in...  40.4 us
    pallas_call x1, Pallas kernels, grads_pass(): pl.pallas_call(grads_kernel, grid=(6,), in_specs=[col(256), full((L, D)),...  18 us
    pallas_call x1, Pallas kernels, gate_pass(): pl.pallas_call(gate_kernel, grid=(L // T,), in_specs=[row(D), full((D, DI...  16.2 us

profile of v1, /device:TPU:0, one launch (start us, length us, event | category | flops | bytes accessed | tf_op | source)
XLA Modules:
  0.0 268.6 jit_solution(3696277216670082612)
XLA Ops:
  0.6 1.4 add_bitcast_fusion.small.head_ref.own_ref
  2.0 70.8 %first_pass.1 = (bf16[2048,768]{1,0:T(8,128)(2,1)}, bf16[768,2048]{1,0:T(8,128)(2,1)}, bf16[768,1920]{1,0:T(8,128)(2,1)}, bf16[2048,1920]{1,0:T(8,128)(2,1)}, bf...) custom-call(bf16[24,3352]{1,0:T(8,128)(2,1)} %w_ref.1, ...), custom_call_target="tpu_custom_call" | custom-call | tf_op jit(solution)/shard_map/first_pass/pallas_call | solution.py:1185
  72.9 16.2 %gate_pass.1 = (bf16[2048,1536]{1,0:T(8,128)(2,1)}, bf16[2048,1536]{1,0:T(8,128)(2,1)}, f32[128,1536]{1,0:T(8,128)}) custom-call(bf16[2048,768]{1,0:T(8,128)(2,1)} %get-tuple-element.63.normed_ref, bf16[768,1536]{1,0:T(8,128)(2,1)} %bitcast.24, bf16[2048,768]{1,0:T(8,128)(2,1)} %bitcast.21, bf16[1536,768]{1,0:T(8,128)(2,1)} %bitcast.26, ...), custom_call_target="tpu_custom_call" | custom-call | tf_op jit(solution)/shard_map/gate_pass/pallas_call | solution.py:386
  89.1 52.5 %second_pass.1 = (bf16[2048,768]{1,0:T(8,128)(2,1)}, bf16[2048,1536]{1,0:T(8,128)(2,1)}, bf16[2048,1536]{1,0:T(8,128)(2,1)}, bf16[2048,1536]{1,0:T(8,128)(2,1)},...) custom-call(bf16[2048,1536]{1,0:T(8,128)(2,1)} %get-tuple-element.69, ...), custom_call_target="tpu_custom_call" | custom-call | tf_op jit(solution)/shard_map/second_pass/pallas_call | solution.py:1221
  141.6 18.0 %grads_pass.1 = (bf16[1536,768]{1,0:T(8,128)(2,1)}, bf16[768,1536]{1,0:T(8,128)(2,1)}, f32[128,1536]{1,0:T(8,128)}) custom-call(bf16[2048,1536]{1,0:T(8,128)(2,1)} %get-tuple-element.86.nout_ref, bf16[2048,768]{1,0:T(8,128)(2,1)} %bitcast.22, bf16[768,2048]{1,0:T(8,128)(2,1)} %get-tuple-element.87.xt_ref.xt_any, ...), custom_call_target="tpu_custom_call" | custom-call | tf_op jit(solution)/shard_map/grads_pass/pallas_call | solution.py:426
  159.5 63.9 %third_pass.1 = (bf16[2048,1920]{1,0:T(8,128)(2,1)}, f32[32,8,128]{2,1,0:T(8,128)}, bf16[16,1920]{1,0:T(8,128)(2,1)}, f32[48,768]{1,0:T(8,128)}, f32[24,1536]{1,0:T(8,128)}) custom-call(bf16[2048,1792]{1,0:T(8,128)(2,1)} %get-tuple-element.71.act_ref, bf16[2048,1920]{1,0:T(8,128)(2,1)} %get-tuple-element.77.convin_ref, ...), custom_call_target="tpu_custom_call" | custom-call | tf_op jit(solution)/shard_map/third_pass/pallas_call | solution.py:1259
  223.4 40.4 %last_pass.1 = (bf16[2048,768]{1,0:T(8,128)(2,1)}, f32[24,1920]{1,0:T(8,128)}, f32[8,128]{1,0:T(8,128)}) custom-call(bf16[768,2048]{1,0:T(8,128)(2,1)} %get-tuple-element.87.xt_ref.xt_any, bf16[2048,1920]{1,0:T(8,128)(2,1)} %get-tuple-element.96.pg_any, bf16[768,1536]{1,0:T(8,128)(2,1)} %bitcast.25, bf16[768,1920]{1,0:T(8,128)(2,1)} %get-tuple-element.97.wc_any, ...), custom_call_target="tpu_custom_call" | custom-call | tf_op jit(solution)/shard_map/last_pass/pallas_call | solution.py:569
  263.8 4.9 %finish_pass.1 = (f32[24,3352]{1,0:T(8,128)}, f32[24]{0:T(128)}, f32[48]{0:T(128)}, f32[4,56]{1,0:T(4,128)}, f32[56]{0:T(128)}, /*index=5*/f32[24]{0:T(128)}, f3...) custom-call(f32[24,1536]{1,0:T(8,128)} %get-tuple-element.95.gate_ref, ...), custom_call_target="tpu_custom_call" | custom-call | tf_op jit(solution)/shard_map/finish_pass/pallas_call | solution.py:632

commit v2 on v1

--- a/solution.py
+++ b/solution.py
@@ -427,11 +427,11 @@
         grads_kernel,
         grid=(6,),
         in_specs=[
-            col(256), full((L, D)), pl.BlockSpec((128, L), lambda i: (i, 0)), full((L, DI)), full((NSTATE, DI)),
+            col(256), once((L, D)), once((D, L)), col(256), full((NSTATE, DI)),
             full((8, BLOCK)),
         ],
         out_specs=[
-            pl.BlockSpec((256, D), lambda i: (i, 0)), pl.BlockSpec((128, DI), lambda i: (i, 0)), full((NSTATE, DI)),
+            pl.BlockSpec((256, D), lambda i: (i, 0)), pl.BlockSpec((D, 256), lambda i: (0, i)), full((NSTATE, DI)),
         ],
         out_shape=[sds((DI, D), BF16), sds((D, DI), BF16), sds((NSTATE, DI), F32)],
         scratch_shapes=[pltpu.VMEM((8, DI), F32)] + chain_scratch(),
@@ -535,12 +535,12 @@
                 sc[k].finish(stage)
                 sc[k].start(stage + 1)
 
-    after(nc + 1, [(3, 0)])
-    after(nc + 3, [(0, 1)])
-    after(nc + 4, [(1, 1)])
-    after(nc + 5, [(2, 1)])
-    after(nc + 6, [(3, 1), (0, 2)])
-    after(nc + 7, [(1, 2), (2, 2), (3, 2)])
+    after(nc, [(3, 0)])
+    after(nc + 1, [(0, 1)])
+    after(nc + 2, [(1, 1)])
+    after(nc + 3, [(2, 1), (0, 2)])
+    after(nc + 4, [(3, 1), (1, 2)])
+    after(nc + 5, [(2, 2), (3, 2)])
 
     @pl.when(i == pl.num_programs(0) - 1)
     def _():
@@ -842,9 +842,8 @@
         def _():
             advance(*what)
 
-    after(2, (6, 2), (7, 2))
-    after(4, (4, 3), (5, 3))
-    after(6, (6, 3), (7, 3))
+    after(4, (6, 2), (7, 2), (4, 3), (5, 3))
+    after(7, (6, 3), (7, 3))
 
     @pl.when(i > 1)
     def _():
@@ -980,7 +979,7 @@
         sca.start(0)
         scb.start(0)
 
-    for stage, when in enumerate((1, 3, 5)):
+    for stage, when in enumerate((1, 4, 6)):
         @pl.when(i == when)
         def _():
             sca.finish(stage)

time: 269 us -> 257 us (0.955)
  Pallas kernels: 267 us -> 255 us
    pallas_call x1, Pallas kernels: 40.4 us -> 34.2 us  [last_pass(): pl.pallas_call(functools.partial(last_kernel, T), grid=(nc + L // T,), in...]
    pallas_call x1, Pallas kernels: 70.8 us -> 67.5 us  [first_pass(): pl.pallas_call(functools.partial(first_kernel, T), grid=(1 + L // T,), in...]
where the time goes in v2:
time: 257 us
  Pallas kernels  255 us (99%)
    pallas_call x1, Pallas kernels, first_pass(): pl.pallas_call(functools.partial(first_kernel, T), grid=(1 + L // T,), in...  67.5 us
    pallas_call x1, Pallas kernels, third_pass(): pl.pallas_call(functools.partial(third_kernel, T), grid=(n,), in_specs=[r...  62.9 us
    pallas_call x1, Pallas kernels, second_pass(): pl.pallas_call(functools.partial(second_kernel, T), grid=(L // T,), in_sp...  52.5 us
    pallas_call x1, Pallas kernels, last_pass(): pl.pallas_call(functools.partial(last_kernel, T), grid=(nc + L // T,), in...  34.2 us
    pallas_call x1, Pallas kernels, grads_pass(): pl.pallas_call(grads_kernel, grid=(6,), in_specs=[col(256), once((L, D)),...  16.9 us
    pallas_call x1, Pallas kernels, gate_pass(): pl.pallas_call(gate_kernel, grid=(L // T,), in_specs=[row(D), full((D, DI...  16.2 us

profile of v2, /device:TPU:0, one launch (start us, length us, event | category | flops | bytes accessed | tf_op | source)
XLA Modules:
  0.0 257.1 jit_solution(11743433671582920135)
XLA Ops:
  0.6 1.4 add_bitcast_fusion.small.head_ref.own_ref
  2.0 67.5 %first_pass.1 = (bf16[2048,768]{1,0:T(8,128)(2,1)}, bf16[768,2048]{1,0:T(8,128)(2,1)}, bf16[768,1920]{1,0:T(8,128)(2,1)}, bf16[2048,1920]{1,0:T(8,128)(2,1)}, bf...) custom-call(bf16[24,3352]{1,0:T(8,128)(2,1)} %w_ref.1, ...), custom_call_target="tpu_custom_call" | custom-call | tf_op jit(solution)/shard_map/first_pass/pallas_call | solution.py:1184
  69.6 16.2 %gate_pass.1 = (bf16[2048,1536]{1,0:T(8,128)(2,1)}, bf16[2048,1536]{1,0:T(8,128)(2,1)}, f32[128,1536]{1,0:T(8,128)}) custom-call(bf16[2048,768]{1,0:T(8,128)(2,1)} %get-tuple-element.63.normed_ref, bf16[768,1536]{1,0:T(8,128)(2,1)} %bitcast.24, bf16[2048,768]{1,0:T(8,128)(2,1)} %bitcast.21, bf16[1536,768]{1,0:T(8,128)(2,1)} %bitcast.26, ...), custom_call_target="tpu_custom_call" | custom-call | tf_op jit(solution)/shard_map/gate_pass/pallas_call | solution.py:386
  85.8 52.5 %second_pass.1 = (bf16[2048,768]{1,0:T(8,128)(2,1)}, bf16[2048,1536]{1,0:T(8,128)(2,1)}, bf16[2048,1536]{1,0:T(8,128)(2,1)}, bf16[2048,1536]{1,0:T(8,128)(2,1)},...) custom-call(bf16[2048,1536]{1,0:T(8,128)(2,1)} %get-tuple-element.69, ...), custom_call_target="tpu_custom_call" | custom-call | tf_op jit(solution)/shard_map/second_pass/pallas_call | solution.py:1220
  138.3 16.9 %grads_pass.1 = (bf16[1536,768]{1,0:T(8,128)(2,1)}, bf16[768,1536]{1,0:T(8,128)(2,1)}, f32[128,1536]{1,0:T(8,128)}) custom-call(bf16[2048,1536]{1,0:T(8,128)(2,1)} %get-tuple-element.86.nout_ref, bf16[2048,768]{1,0:T(8,128)(2,1)} %bitcast.22, bf16[768,2048]{1,0:T(8,128)(2,1)} %get-tuple-element.87.xt_ref.xt_any, ...), custom_call_target="tpu_custom_call" | custom-call | tf_op jit(solution)/shard_map/grads_pass/pallas_call | solution.py:426
  155.2 62.9 %third_pass.1 = (bf16[2048,1920]{1,0:T(8,128)(2,1)}, f32[32,8,128]{2,1,0:T(8,128)}, bf16[16,1920]{1,0:T(8,128)(2,1)}, f32[48,768]{1,0:T(8,128)}, f32[24,1536]{1,0:T(8,128)}) custom-call(bf16[2048,1792]{1,0:T(8,128)(2,1)} %get-tuple-element.71.act_ref, bf16[2048,1920]{1,0:T(8,128)(2,1)} %get-tuple-element.77.convin_ref, ...), custom_call_target="tpu_custom_call" | custom-call | tf_op jit(solution)/shard_map/third_pass/pallas_call | solution.py:1258
  218.0 34.2 %last_pass.1 = (bf16[2048,768]{1,0:T(8,128)(2,1)}, f32[24,1920]{1,0:T(8,128)}, f32[8,128]{1,0:T(8,128)}) custom-call(bf16[768,2048]{1,0:T(8,128)(2,1)} %get-tuple-element.87.xt_ref.xt_any, bf16[2048,1920]{1,0:T(8,128)(2,1)} %get-tuple-element.96.pg_any, bf16[768,1536]{1,0:T(8,128)(2,1)} %bitcast.25, bf16[768,1920]{1,0:T(8,128)(2,1)} %get-tuple-element.97.wc_any, ...), custom_call_target="tpu_custom_call" | custom-call | tf_op jit(solution)/shard_map/last_pass/pallas_call | solution.py:569
  252.2 4.9 %finish_pass.1 = (f32[24,3352]{1,0:T(8,128)}, f32[24]{0:T(128)}, f32[48]{0:T(128)}, f32[4,56]{1,0:T(4,128)}, f32[56]{0:T(128)}, /*index=5*/f32[24]{0:T(128)}, f3...) custom-call(f32[24,1536]{1,0:T(8,128)} %get-tuple-element.95.gate_ref, ...), custom_call_target="tpu_custom_call" | custom-call | tf_op jit(solution)/shard_map/finish_pass/pallas_call | solution.py:632

commit v3 on v2

--- a/solution.py
+++ b/solution.py
@@ -537,10 +537,9 @@
 
     after(nc, [(3, 0)])
     after(nc + 1, [(0, 1)])
-    after(nc + 2, [(1, 1)])
-    after(nc + 3, [(2, 1), (0, 2)])
-    after(nc + 4, [(3, 1), (1, 2)])
-    after(nc + 5, [(2, 2), (3, 2)])
+    after(nc + 2, [(1, 1), (2, 1), (0, 2)])
+    after(nc + 3, [(3, 1), (1, 2)])
+    after(nc + 4, [(2, 2), (3, 2)])
 
     @pl.when(i == pl.num_programs(0) - 1)
     def _():

time: 257 us -> 258 us (level)
  no operation moved by 1% of the time
where the time goes in v3:
time: 258 us
  Pallas kernels  256 us (99%)
    pallas_call x1, Pallas kernels, first_pass(): pl.pallas_call(functools.partial(first_kernel, T), grid=(1 + L // T,), in...  67.5 us
    pallas_call x1, Pallas kernels, third_pass(): pl.pallas_call(functools.partial(third_kernel, T), grid=(n,), in_specs=[r...  62.9 us
    pallas_call x1, Pallas kernels, second_pass(): pl.pallas_call(functools.partial(second_kernel, T), grid=(L // T,), in_sp...  52.5 us
    pallas_call x1, Pallas kernels, last_pass(): pl.pallas_call(functools.partial(last_kernel, T), grid=(nc + L // T,), in...  34.8 us
    pallas_call x1, Pallas kernels, grads_pass(): pl.pallas_call(grads_kernel, grid=(6,), in_specs=[col(256), once((L, D)),...  16.9 us
    pallas_call x1, Pallas kernels, gate_pass(): pl.pallas_call(gate_kernel, grid=(L // T,), in_specs=[row(D), full((D, DI...  16.2 us

profile of v3, /device:TPU:0, one launch (start us, length us, event | category | flops | bytes accessed | tf_op | source)
XLA Modules:
  0.0 257.7 jit_solution(6213398019264232306)
XLA Ops:
  0.6 1.4 add_bitcast_fusion.small.head_ref.own_ref
  2.0 67.5 %first_pass.1 = (bf16[2048,768]{1,0:T(8,128)(2,1)}, bf16[768,2048]{1,0:T(8,128)(2,1)}, bf16[768,1920]{1,0:T(8,128)(2,1)}, bf16[2048,1920]{1,0:T(8,128)(2,1)}, bf...) custom-call(bf16[24,3352]{1,0:T(8,128)(2,1)} %w_ref.1, ...), custom_call_target="tpu_custom_call" | custom-call | tf_op jit(solution)/shard_map/first_pass/pallas_call | solution.py:1183
  69.6 16.2 %gate_pass.1 = (bf16[2048,1536]{1,0:T(8,128)(2,1)}, bf16[2048,1536]{1,0:T(8,128)(2,1)}, f32[128,1536]{1,0:T(8,128)}) custom-call(bf16[2048,768]{1,0:T(8,128)(2,1)} %get-tuple-element.63.normed_ref, bf16[768,1536]{1,0:T(8,128)(2,1)} %bitcast.24, bf16[2048,768]{1,0:T(8,128)(2,1)} %bitcast.21, bf16[1536,768]{1,0:T(8,128)(2,1)} %bitcast.26, ...), custom_call_target="tpu_custom_call" | custom-call | tf_op jit(solution)/shard_map/gate_pass/pallas_call | solution.py:386
  85.8 52.5 %second_pass.1 = (bf16[2048,768]{1,0:T(8,128)(2,1)}, bf16[2048,1536]{1,0:T(8,128)(2,1)}, bf16[2048,1536]{1,0:T(8,128)(2,1)}, bf16[2048,1536]{1,0:T(8,128)(2,1)},...) custom-call(bf16[2048,1536]{1,0:T(8,128)(2,1)} %get-tuple-element.69, ...), custom_call_target="tpu_custom_call" | custom-call | tf_op jit(solution)/shard_map/second_pass/pallas_call | solution.py:1219
  138.3 16.9 %grads_pass.1 = (bf16[1536,768]{1,0:T(8,128)(2,1)}, bf16[768,1536]{1,0:T(8,128)(2,1)}, f32[128,1536]{1,0:T(8,128)}) custom-call(bf16[2048,1536]{1,0:T(8,128)(2,1)} %get-tuple-element.86.nout_ref, bf16[2048,768]{1,0:T(8,128)(2,1)} %bitcast.22, bf16[768,2048]{1,0:T(8,128)(2,1)} %get-tuple-element.87.xt_ref.xt_any, ...), custom_call_target="tpu_custom_call" | custom-call | tf_op jit(solution)/shard_map/grads_pass/pallas_call | solution.py:426
  155.2 62.9 %third_pass.1 = (bf16[2048,1920]{1,0:T(8,128)(2,1)}, f32[32,8,128]{2,1,0:T(8,128)}, bf16[16,1920]{1,0:T(8,128)(2,1)}, f32[48,768]{1,0:T(8,128)}, f32[24,1536]{1,0:T(8,128)}) custom-call(bf16[2048,1792]{1,0:T(8,128)(2,1)} %get-tuple-element.71.act_ref, bf16[2048,1920]{1,0:T(8,128)(2,1)} %get-tuple-element.77.convin_ref, ...), custom_call_target="tpu_custom_call" | custom-call | tf_op jit(solution)/shard_map/third_pass/pallas_call | solution.py:1257
  218.0 34.8 %last_pass.1 = (bf16[2048,768]{1,0:T(8,128)(2,1)}, f32[24,1920]{1,0:T(8,128)}, f32[8,128]{1,0:T(8,128)}) custom-call(bf16[768,2048]{1,0:T(8,128)(2,1)} %get-tuple-element.87.xt_ref.xt_any, bf16[2048,1920]{1,0:T(8,128)(2,1)} %get-tuple-element.96.pg_any, bf16[768,1536]{1,0:T(8,128)(2,1)} %bitcast.25, bf16[768,1920]{1,0:T(8,128)(2,1)} %get-tuple-element.97.wc_any, ...), custom_call_target="tpu_custom_call" | custom-call | tf_op jit(solution)/shard_map/last_pass/pallas_call | solution.py:568
  252.9 4.9 %finish_pass.1 = (f32[24,3352]{1,0:T(8,128)}, f32[24]{0:T(128)}, f32[48]{0:T(128)}, f32[4,56]{1,0:T(4,128)}, f32[56]{0:T(128)}, /*index=5*/f32[24]{0:T(128)}, f3...) custom-call(f32[24,1536]{1,0:T(8,128)} %get-tuple-element.95.gate_ref, ...), custom_call_target="tpu_custom_call" | custom-call | tf_op jit(solution)/shard_map/finish_pass/pallas_call | solution.py:631
